TPU v7x, 256 devices: a whole 4x4x8 slice. The times are simulated.
256 devices in a mesh: slab: 8 (over x, core), tile: 32 (over z, y).
Axes of the slice: x: 4, y: 4, z: 8, core: 2. Of those that a mesh axis runs over, the one named last changes fastest.
Arguments:
- positions: float32 [3, 16384, 128], P(None, ('slab', 'tile')), may hold values from 0 to 1.6
- velocities: float32 [3, 16384, 128], P(None, ('slab', 'tile')), may hold values from -6 to 6
- masses: float32 [16384, 128], P(('slab', 'tile')), may hold values from 0.01 to 0.1
- wall_areas: float32 [16384, 128], P(('slab', 'tile')), may hold values from 0.02 to 0.2
- normals: float32 [3, 16384, 128], P(None, ('slab', 'tile')), may hold values from -1 to 1, as said below
- wall_flags: int32 [16384], P(('slab', 'tile')), may hold values 0 or 1
- counts: int32 [16384], P(('slab', 'tile')), may hold values from 1 to 128, as said below
- send_list: int32 [256, 32, 4], P(('slab', 'tile')), may hold values from 0 to 63, as said below
- local_pairs: int32 [16384, 2], P(('slab', 'tile')), may hold values from 0 to 63, as said below
- remote_pairs: int32 [40960, 2], P(('slab', 'tile')), may hold values from 0 to 223, as said below
- remote_live: int32 [256], P(('slab', 'tile')), may hold values from 40 to 160, as said below
Outputs:
- density: float32 [16384, 128], P(('slab', 'tile'))
- acceleration: float32 [3, 16384, 128], P(None, ('slab', 'tile'))
Inputs may be any that keep to these rules, and one draw needn't show every extreme that they name: `counts`: every device has one block holding 128 particles; slots at or after a block's count are empty. `normals`: every component is 0.2 or more in magnitude. `send_list`: own block numbers of the sending device, distinct within the 4 entries for one receiving device. `local_pairs`: the two blocks of a row differ. `remote_pairs`: column 0 is an own block number below 64; column 1 is below 16 only for devices not in the first slab, between 80 and 95 only for devices not in the last slab, otherwise 64 + 2 * 16 or more with p never the device's own tile. `remote_live`: some device has all 160 rows live.
All inputs are finite; a program needn't handle non-finite values. No bound on the sum of `wall_flags` on one device may be relied on, other than what follows from the above.
Results may differ from a plain program's by a relative error of at most 0.00002.
Values sent between devices are 32-bit elements; how exact they have to be, the bound alone decides.
No kernel may reach another device: no remote copies, remote signals or barrier semaphores. Data moves between devices by JAX's collectives and lax.ppermute only.
A program may use at most 64 MiB of HBM per device.

v0:
```python
import functools
import math

import jax
import jax.numpy as jnp
from jax import lax
from jax.experimental import pallas as pl
from jax.experimental.pallas import tpu as pltpu
from jax.sharding import PartitionSpec as P

kernel_norm = 21.0 / (16.0 * math.pi)
softening = 0.01
tiny = 1e-30
lanes = 128
rows_item = 32
groups = rows_item // 8
batch = lanes // rows_item
halves = 2
field_order = (0, 1, 2, 6, 3, 4, 5, 7)
bf16 = jnp.bfloat16
vmem = pltpu.VMEM
smem = pltpu.SMEM


def spec(space):
    return pl.BlockSpec(memory_space=space)


def params(mib):
    return pltpu.CompilerParams(vmem_limit_bytes=mib * 1024 * 1024)


def column_of(row):
    number = row.shape[1]
    same = lax.broadcasted_iota(jnp.int32, (number, number), 0) == lax.broadcasted_iota(
        jnp.int32, (number, number), 1
    )
    return jnp.sum(jnp.where(same, row, 0.0), axis=1, keepdims=True)


def pack_kernel(
    blocks, faces, per_peer, send, pos, vel, mass, area, normal, flags_row, counts_row, table, picked, head, tail
):
    slot = lax.broadcasted_iota(jnp.int32, (blocks, lanes), 1).astype(jnp.float32)
    alive = slot < column_of(counts_row[...].astype(jnp.float32))
    wall_value = column_of(flags_row[...].astype(jnp.float32)) + jnp.zeros((blocks, lanes), jnp.float32)
    wall = wall_value > 0.5
    nx, ny, nz = normal[0], normal[1], normal[2]
    length = jnp.sqrt(nx * nx + ny * ny + nz * nz)
    weight = jnp.where(alive, jnp.where(wall, area[...], mass[...]), 0.0)
    wall_scale = weight / length
    parts = (nx, ny, nz)
    for c in range(3):
        table[pl.ds(c, blocks, stride=8), :] = 0.5 * pos[c]
        table[pl.ds(3 + c, blocks, stride=8), :] = jnp.where(wall, wall_scale * parts[c], vel[c])
    table[pl.ds(6, blocks, stride=8), :] = weight
    table[pl.ds(7, blocks, stride=8), :] = wall_value
    head[...] = table[0 : faces * 8, :]
    tail[...] = table[(blocks - faces) * 8 : blocks * 8, :]

    def pick(t, carry):
        for k in range(per_peer):
            source = pl.multiple_of(send[0, t, k] * 8, 8)
            at = pl.multiple_of((t * per_peer + k) * 8, 8)
            picked[pl.ds(at, 8), :] = table[pl.ds(source, 8), :]
        return carry

    lax.fori_loop(0, picked.shape[0] // (8 * per_peer), pick, 0, unroll=2)


def rounded(x):
    return x.astype(bf16).astype(jnp.float32)


def split3(x):
    high = rounded(x)
    rest = x - high
    middle = rounded(rest)
    return high, middle, rest - middle


def make_spread(spread):
    shape = spread.shape
    k = lax.broadcasted_iota(jnp.int32, shape, 0) & 31
    tile = lax.broadcasted_iota(jnp.int32, shape, 1) >> 7
    want = jnp.where(tile == 3, 6, jnp.where(tile > 3, tile - 1, tile))
    want = jnp.where(tile == 7, 7, want)
    hit = jnp.logical_and(jnp.logical_and(k < 24, (k & 7) == want), tile < 8)
    hit = jnp.logical_or(hit, jnp.logical_and(jnp.logical_and(k >= 24, k < 27), tile == 8))
    spread[...] = jnp.where(hit, 1.0, 0.0).astype(bf16)


def make_columns(blocks, table, last, columns, stage):
    lane = lax.broadcasted_iota(jnp.int32, (lanes, lanes), 1) >> 5
    for g in range(blocks // 4):
        for j in range(4):
            b = 4 * g + j
            for p, piece in enumerate(split3(table[8 * b : 8 * b + 8, :])):
                stage[32 * b + 8 * p : 32 * b + 8 * p + 8, :] = piece
            if last is None:
                stage[32 * b + 24 : 32 * b + 32, :] = jnp.zeros((8, lanes), jnp.float32)
            else:
                stage[32 * b + 24 : 32 * b + 32, :] = last[8 * b : 8 * b + 8, :]

    def some(g, carry):
        turned = stage[pl.ds(pl.multiple_of(g * lanes, lanes), lanes), :].T
        for j in range(4):
            columns[g * 4 + j] = jnp.where(lane == j, turned, 0.0).astype(bf16)
        return carry

    lax.fori_loop(0, blocks // 4, some, 0)
    columns[blocks] = jnp.zeros((lanes, lanes), bf16)


def put_items(items, at, first, second):
    code = first | (second << 8)
    for k in range(lanes // rows_item):
        items[at + k] = code | (k << 16)


def close_items(items, count, blocks):
    for k in range(batch * halves):
        items[count + k] = jnp.int32(blocks)


def decode(code):
    first = code & 255
    second = (code >> 8) & 255
    row = pl.multiple_of((code >> 16) * rows_item, rows_item)
    return first, second, row


def wide(row):
    return jnp.broadcast_to(row, (8, lanes))


def spread_fields(columns, spread, wide_fields, tiles, decoded):
    left = jnp.concatenate([columns[first, pl.ds(row, rows_item), :] for first, second, row in decoded], axis=0)
    for t in range((tiles + 1) // 2):
        both = jnp.dot(left, spread[:, 256 * t : 256 * t + 256], preferred_element_type=jnp.float32)
        wide_fields[2 * t] = both[:, 0:lanes]
        wide_fields[2 * t + 1] = both[:, lanes : 2 * lanes]


def close_u(fields, rows):
    dx = fields[0] - rows[0]
    dy = fields[1] - rows[1]
    dz = fields[2] - rows[2]
    square = dx * dx + dy * dy + dz * dz
    safe = jnp.maximum(square, tiny)
    q = safe * lax.rsqrt(safe)
    u = jnp.maximum(1.0 - q, 0.0)
    return dx, dy, dz, square, u


def kernel_shape(u):
    u2 = u * u
    return (u2 * u2) * (5.0 - 4.0 * u)


def run_items(columns, spread, wide_fields, tiles, items, count, body, finish):
    def step(it, carry):
        done = []
        for h in range(halves):
            decoded = [decode(items[(it * halves + h) * batch + k]) for k in range(batch)]
            spread_fields(columns, spread, wide_fields[h], tiles, decoded)
            done.append((decoded, body(wide_fields[h], decoded)))
        for decoded, outs in done:
            finish(decoded, outs)
        return carry

    size = batch * halves
    lax.fori_loop(0, (count + size - 1) // size, step, 0)


def merge_lanes(values, first, lane):
    base = (first & 15) * 8
    total = jnp.zeros((8, lanes), jnp.float32)
    for c, value in enumerate(values):
        total = jnp.where(lane == base + c, value, total)
    return total


def merge_rows(values, sub):
    total = jnp.zeros((8, lanes), jnp.float32)
    for c, value in enumerate(values):
        total = jnp.where(sub == c, jnp.sum(value, axis=0, keepdims=True), total)
    return total


def add_sums(acc_first, acc_second, decoded, outs):
    for (first, second, row), (merged, tile) in zip(decoded, outs):
        if merged:
            slab = first >> 4
            for g in range(groups):
                acc_first[slab, pl.ds(row + 8 * g, 8), :] += merged[g]
        if tile is not None:
            at = pl.multiple_of(second * 8, 8)
            acc_second[pl.ds(at, 8), :] += tile


def density_body(source, to_first, to_second, wide_fields, decoded):
    lane = lax.broadcasted_iota(jnp.int32, (8, lanes), 1)
    sub = lax.broadcasted_iota(jnp.int32, (8, lanes), 0)
    outs = []
    for k, (first, second, row) in enumerate(decoded):
        base = pl.multiple_of(second * 8, 8)
        rows = [wide(source[pl.ds(base + c, 1), :]) for c in range(3)]
        given = []
        if to_first:
            given = [wide(source[pl.ds(base + 6, 1), :])]
            if to_first == 4:
                given += [wide(source[pl.ds(base + 3 + c, 1), :]) for c in range(3)]
        merged = []
        sums = None
        for g in range(groups):
            at = rows_item * k + 8 * g
            fields = [wide_fields[f, at : at + 8, :] for f in range(3 + to_second)]
            w = kernel_shape(close_u(fields, rows)[4])
            if to_first:
                values = [jnp.sum(w * other, axis=1, keepdims=True) for other in given]
                merged.append(merge_lanes(values, first, lane))
            if to_second:
                back = [w * field for field in fields[3:]]
                sums = back if sums is None else [s + b for s, b in zip(sums, back)]
        outs.append((merged, merge_rows(sums, sub) if to_second else None))
    return outs


def clear(ref, pieces):
    size = ref.shape[0] // pieces

    def some(k, carry):
        at = pl.multiple_of(k * size, size)
        ref[pl.ds(at, size)] = jnp.zeros((size,) + tuple(ref.shape[1:]), jnp.float32)
        return carry

    lax.fori_loop(0, pieces, some, 0)


def plane(ref, number, c):
    return ref[pl.ds(c, number, stride=8), :]


def first_rows(acc_first, turned, blocks):
    for s in range(blocks // 16):
        turned[s * lanes : (s + 1) * lanes, :] = acc_first[s].T


def run_density(columns, spread, fields, source, acc_first, acc_second, to_first, to_second, items, count):
    run_items(
        columns,
        spread,
        fields,
        3 + to_second,
        items,
        count,
        functools.partial(density_body, source, to_first, to_second),
        functools.partial(add_sums, acc_first, acc_second),
    )


def self_density_kernel(
    blocks, counts, flags, table, columns, own, items, stage, spread, wide_a, wide_b, acc_second
):
    make_columns(blocks, table, None, columns, stage)
    make_spread(spread)
    clear(acc_second, 4)

    def self_step(b, n):
        put_items(items, n, b, b)
        return n + jnp.where(flags[b] > 0, 0, (counts[b] + rows_item - 1) // rows_item)

    count = lax.fori_loop(0, blocks, self_step, jnp.int32(0), unroll=4)
    close_items(items, count, blocks)
    items[items.shape[0] - 1] = count
    run_density(columns, spread, (wide_a, wide_b), table, None, acc_second, 0, 1, items, count)
    own[...] = plane(acc_second, blocks, 0)


def local_density_kernel(
    blocks,
    counts,
    flags,
    pairs,
    table,
    columns,
    own,
    both_items,
    spread,
    wide_a,
    wide_b,
    acc_first,
    acc_second,
    turned,
    wall_items,
):
    make_spread(spread)
    clear(acc_first, 1)
    clear(acc_second, 4)

    def pair_step(p, carry):
        n_both, n_wall = carry
        a = pairs[0, p]
        b = pairs[1, p]
        kinds = flags[a] + flags[b]
        swap = jnp.where(kinds == 1, flags[b] > 0, counts[b] < counts[a])
        first = jnp.where(swap, b, a)
        second = jnp.where(swap, a, b)
        number = (counts[first] + rows_item - 1) // rows_item
        put_items(both_items, n_both, first, second)
        put_items(wall_items, n_wall, first, second)
        return (n_both + jnp.where(kinds == 0, number, 0), n_wall + jnp.where(kinds == 1, number, 0))

    n_both, n_wall = lax.fori_loop(
        0, pairs.shape[1], pair_step, (jnp.int32(0), jnp.int32(0)), unroll=4
    )
    close_items(both_items, n_both, blocks)
    close_items(wall_items, n_wall, blocks)
    both_items[both_items.shape[0] - 1] = n_both
    density = functools.partial(
        run_density, columns, spread, (wide_a, wide_b), table, acc_first, acc_second
    )
    density(1, 1, both_items, n_both)
    density(0, 4, wall_items, n_wall)
    first_rows(acc_first, turned, blocks)
    for c in range(4):
        own[c] = plane(turned, blocks, c) + plane(acc_second, blocks, c)


def far_density_kernel(
    blocks,
    faces,
    counts,
    flags,
    live,
    pairs,
    columns,
    low,
    high,
    far,
    own,
    back_low,
    back_high,
    back_far,
    push,
    both_items,
    spread,
    wide_a,
    wide_b,
    acc_first,
    acc_second,
    turned,
    source,
    wall_rows,
    wall_flag,
    first_items,
    second_items,
    sem,
):
    others = source.shape[0] // 8
    source[0 : faces * 8, :] = low[...]
    source[faces * 8 : 2 * faces * 8, :] = high[...]
    source[2 * faces * 8 :, :] = far[...]
    wall_rows[...] = plane(source, others, 7)
    copy = pltpu.make_async_copy(wall_rows, wall_flag, sem)
    copy.start()
    make_spread(spread)
    clear(acc_first, 1)
    clear(acc_second, 4)
    copy.wait()

    def pair_step(p, carry):
        n_both, n_first, n_second = carry
        a = pairs[0, p]
        j = pairs[1, p]
        b = jnp.where(j < blocks, j, j - blocks)
        wall_a = flags[a]
        wall_b = jnp.where(wall_flag[b, 0] > 0.5, 1, 0)
        number = jnp.where(p < live[0], (counts[a] + rows_item - 1) // rows_item, 0)
        put_items(both_items, n_both, a, b)
        put_items(first_items, n_first, a, b)
        put_items(second_items, n_second, a, b)
        return (
            n_both + number * (1 - wall_a) * (1 - wall_b),
            n_first + number * (1 - wall_a) * wall_b,
            n_second + number * wall_a * (1 - wall_b),
        )

    zero = jnp.int32(0)
    n_both, n_first, n_second = lax.fori_loop(
        0, pairs.shape[1], pair_step, (zero, zero, zero), unroll=4
    )
    close_items(both_items, n_both, blocks)
    close_items(first_items, n_first, blocks)
    close_items(second_items, n_second, blocks)
    both_items[both_items.shape[0] - 1] = n_both
    density = functools.partial(
        run_density, columns, spread, (wide_a, wide_b), source, acc_first, acc_second
    )
    density(1, 1, both_items, n_both)
    density(4, 0, first_items, n_first)
    density(0, 4, second_items, n_second)
    first_rows(acc_first, turned, blocks)
    for c in range(4):
        own[c] = plane(turned, blocks, c)
    back_low[...] = acc_second[pl.ds(0, faces, stride=8), :]
    back_high[...] = acc_second[pl.ds(faces * 8, faces, stride=8), :]
    back_far[...] = acc_second[pl.ds(2 * faces * 8, others - 2 * faces, stride=8), :]
    for c in range(3):
        push[c] = plane(acc_second, others, 1 + c)


def fluid_mask(blocks, table):
    return jnp.logical_and(plane(table, blocks, 6) > 0.0, plane(table, blocks, 7) < 0.5)


def density_kernel(
    blocks,
    faces,
    per_peer,
    send,
    table,
    self_sum,
    local_sum,
    far_sum,
    from_above,
    from_below,
    returned,
    density,
    picked,
    head,
    tail,
):
    density[...] = self_sum[...] + local_sum[0] + far_sum[0]
    density[blocks - faces :, :] += from_above[...]
    density[0:faces, :] += from_below[...]
    peers = picked.shape[0] // per_peer

    def give(t, carry):
        for k in range(per_peer):
            density[pl.ds(send[0, t, k], 1), :] += returned[pl.ds(t * per_peer + k, 1), :]
        return carry

    lax.fori_loop(0, peers, give, 0, unroll=2)
    density[...] = jnp.where(fluid_mask(blocks, table), kernel_norm * density[...], 0.0)
    head[...] = density[0:faces, :]
    tail[...] = density[blocks - faces :, :]

    def pick(t, carry):
        for k in range(per_peer):
            picked[pl.ds(t * per_peer + k, 1), :] = density[pl.ds(send[0, t, k], 1), :]
        return carry

    lax.fori_loop(0, peers, pick, 0, unroll=4)


def force_fields(source, density, number, pressed):
    mass = plane(source, number, 6)
    rho = jnp.where(mass > 0.0, density, 1.0)
    inverse = 1.0 / jnp.where(rho > 0.0, rho, 1.0)
    scaled = mass * inverse
    source[pl.ds(7, number, stride=8), :] = scaled
    press = 10.0 * (rho - 1.0) * inverse * scaled
    pressed[...] = press
    return press


def force_body(source, pressed, to_first, wide_fields, decoded):
    lane = lax.broadcasted_iota(jnp.int32, (8, lanes), 1)
    sub = lax.broadcasted_iota(jnp.int32, (8, lanes), 0)
    outs = []
    for k, (first, second, row) in enumerate(decoded):
        base = pl.multiple_of(second * 8, 8)
        rows = [wide(source[pl.ds(base + c, 1), :]) for c in range(8)]
        press = wide(pressed[pl.ds(second, 1), :])
        merged = []
        sums = None
        for g in range(groups):
            at = rows_item * k + 8 * g
            fields = [wide_fields[f, at : at + 8, :] for f in range(9)]
            dx, dy, dz, square, u = close_u(fields, rows)
            u3 = (u * u) * u
            damp = u3 * (square * (1.0 / (square + 0.25 * softening))) * (fields[7] * rows[7])
            pull = u3 * (fields[8] * rows[6] + fields[3] * press)
            values = [
                pull * d - damp * (fields[4 + c] - rows[3 + c]) for c, d in enumerate((dx, dy, dz))
            ]
            if to_first:
                merged.append(
                    merge_lanes([jnp.sum(v, axis=1, keepdims=True) for v in values], first, lane)
                )
            sums = values if sums is None else [s + v for s, v in zip(sums, values)]
        outs.append((merged, merge_rows(sums, sub)))
    return outs


def run_force(columns, spread, fields, source, pressed, acc_first, acc_second, to_first, items):
    run_items(
        columns,
        spread,
        fields,
        9,
        items,
        items[items.shape[0] - 1],
        functools.partial(force_body, source, pressed, to_first),
        functools.partial(add_sums, acc_first, acc_second),
    )


def self_force_kernel(
    blocks,
    items,
    table,
    density,
    columns,
    source,
    pressed,
    own,
    stage,
    last,
    spread,
    wide_a,
    wide_b,
    acc_second,
):
    source[...] = table[...]
    press = force_fields(source, density[...], blocks, pressed)
    last[...] = jnp.zeros(last.shape, jnp.float32)
    for p, piece in enumerate(split3(press)):
        last[pl.ds(p, blocks, stride=8), :] = piece
    make_columns(blocks, source, last, columns, stage)
    make_spread(spread)
    clear(acc_second, 4)
    run_force(columns, spread, (wide_a, wide_b), source, pressed, None, acc_second, False, items)
    for c in range(3):
        own[c] = -plane(acc_second, blocks, c)


def local_force_kernel(
    blocks,
    items,
    columns,
    source,
    pressed,
    own,
    spread,
    wide_a,
    wide_b,
    acc_first,
    acc_second,
    turned,
):
    make_spread(spread)
    clear(acc_first, 1)
    clear(acc_second, 4)
    run_force(columns, spread, (wide_a, wide_b), source, pressed, acc_first, acc_second, True, items)
    first_rows(acc_first, turned, blocks)
    for c in range(3):
        own[c] = plane(turned, blocks, c) - plane(acc_second, blocks, c)


def far_force_kernel(
    blocks,
    faces,
    items,
    columns,
    low,
    high,
    far,
    low_density,
    high_density,
    far_density,
    push,
    own,
    back_low,
    back_high,
    back_far,
    source,
    source_density,
    pressed,
    spread,
    wide_a,
    wide_b,
    acc_first,
    acc_second,
    turned,
):
    others = source.shape[0] // 8
    source[0 : faces * 8, :] = low[...]
    source[faces * 8 : 2 * faces * 8, :] = high[...]
    source[2 * faces * 8 :, :] = far[...]
    source_density[0:faces, :] = low_density[...]
    source_density[faces : 2 * faces, :] = high_density[...]
    source_density[2 * faces :, :] = far_density[...]
    mass = plane(source, others, 6)
    inverse = 1.0 / jnp.where(mass > 0.0, mass, 1.0)
    force_fields(source, source_density[...], others, pressed)
    make_spread(spread)
    clear(acc_first, 1)
    clear(acc_second, 4)
    run_force(columns, spread, (wide_a, wide_b), source, pressed, acc_first, acc_second, True, items)
    first_rows(acc_first, turned, blocks)
    for c in range(3):
        own[c] = plane(turned, blocks, c)
        acc_second[pl.ds(c, others, stride=8), :] = push[c] - plane(acc_second, others, c) * inverse
    for at, (out, number) in zip(
        (0, faces, 2 * faces), ((back_low, faces), (back_high, faces), (back_far, others - 2 * faces))
    ):
        for k in range(number):
            out[4 * k : 4 * k + 4, :] = acc_second[8 * (at + k) : 8 * (at + k) + 4, :]


def final_kernel(
    blocks,
    faces,
    per_peer,
    send,
    table,
    local_sum,
    far_sum,
    self_force,
    local_force,
    far_force,
    from_above,
    from_below,
    returned,
    out,
    total,
):
    mass = plane(table, blocks, 6)
    inverse = 1.0 / jnp.where(mass > 0.0, mass, 1.0)
    for c in range(3):
        force = (self_force[c] + local_force[c] + far_force[c]) * inverse
        total[pl.ds(c, blocks, stride=8), :] = local_sum[1 + c] + far_sum[1 + c] + force
    for k in range(faces):
        at = 8 * (blocks - faces + k)
        total[at : at + 4, :] += from_above[4 * k : 4 * k + 4, :]
        total[8 * k : 8 * k + 4, :] += from_below[4 * k : 4 * k + 4, :]

    def give(t, carry):
        for k in range(per_peer):
            at = pl.multiple_of(send[0, t, k] * 8, 8)
            source = pl.multiple_of((t * per_peer + k) * 4, 4)
            total[pl.ds(at, 4), :] += returned[pl.ds(source, 4), :]
        return carry

    lax.fori_loop(0, send.shape[1], give, 0, unroll=2)
    fluid = fluid_mask(blocks, table)
    for c in range(3):
        out[c] = jnp.where(fluid, kernel_norm * plane(total, blocks, c), 0.0)


def f32(*shape):
    return jax.ShapeDtypeStruct(shape, jnp.float32)


def i32(*shape):
    return jax.ShapeDtypeStruct(shape, jnp.int32)


def to_above(shard):
    count = lax.axis_size("slab")
    return lax.ppermute(shard, "slab", [(i, i + 1) for i in range(count - 1)])


def to_below(shard):
    count = lax.axis_size("slab")
    return lax.ppermute(shard, "slab", [(i + 1, i) for i in range(count - 1)])


def swap_tiles(rows, tiles):
    parts = rows.reshape(tiles, rows.shape[0] // tiles, lanes)
    return lax.all_to_all(parts, "tile", split_axis=0, concat_axis=0, tiled=True).reshape(rows.shape)


def on_device(
    positions,
    velocities,
    masses,
    wall_areas,
    normals,
    wall_flags,
    counts,
    send_list,
    local_pairs,
    remote_pairs,
    remote_live,
):
    blocks = positions.shape[1]
    faces = blocks // 4
    tiles = lax.axis_size("tile")
    per_peer = send_list.shape[2]
    offered = send_list.shape[1] * per_peer
    others = 2 * faces + offered
    n_local = local_pairs.shape[0]
    n_remote = remote_pairs.shape[0]
    per = lanes // rows_item
    spare = 2 * batch * halves
    self_cap = per * blocks + spare
    own_cap = per * n_local + spare
    far_cap = per * n_remote + spare
    columns_shape = jax.ShapeDtypeStruct((blocks + 1, lanes, lanes), bf16)
    stage = vmem((blocks * 32, lanes), jnp.float32)

    def fields(number):
        return [vmem((lanes, 128 * number), bf16)] + [vmem((number, lanes, lanes), jnp.float32)] * 2

    def sums(number):
        return [
            vmem((blocks // 16 + 1, lanes, lanes), jnp.float32),
            vmem((number * 8, lanes), jnp.float32),
            vmem((blocks * 8, lanes), jnp.float32),
        ]

    def cost(flops):
        return pl.CostEstimate(flops=flops, bytes_accessed=400_000, transcendentals=0)

    table, picked, head, tail = pl.pallas_call(
        functools.partial(pack_kernel, blocks, faces, per_peer),
        out_shape=(f32(blocks * 8, lanes), f32(offered * 8, lanes), f32(faces * 8, lanes), f32(faces * 8, lanes)),
        in_specs=[spec(smem)] + [spec(vmem)] * 7,
        out_specs=[spec(vmem)] * 4,
        name="pack",
    )(
        send_list,
        positions,
        velocities,
        masses,
        wall_areas,
        normals,
        wall_flags[None, :],
        counts[None, :],
    )
    low = to_above(tail)
    high = to_below(head)
    far = swap_tiles(picked, tiles)

    columns, self_sum, self_items = pl.pallas_call(
        functools.partial(self_density_kernel, blocks),
        out_shape=(columns_shape, f32(blocks, lanes), i32(self_cap)),
        in_specs=[spec(smem)] * 2 + [spec(vmem)],
        out_specs=[spec(vmem), spec(vmem), spec(smem)],
        scratch_shapes=[stage] + fields(8) + [vmem((blocks * 8, lanes), jnp.float32)],
        compiler_params=params(20),
        cost_estimate=cost(40_000_000),
        name="self_density",
    )(counts, wall_flags, table)

    far_sum, back_low, back_high, back_far, push, far_items = pl.pallas_call(
        functools.partial(far_density_kernel, blocks, faces),
        out_shape=(
            f32(4, blocks, lanes),
            f32(faces, lanes),
            f32(faces, lanes),
            f32(offered, lanes),
            f32(3, others, lanes),
            i32(far_cap),
        ),
        in_specs=[spec(smem)] * 4 + [spec(vmem)] * 4,
        out_specs=[spec(vmem)] * 5 + [spec(smem)],
        scratch_shapes=fields(8)
        + sums(others)
        + [
            vmem((others * 8, lanes), jnp.float32),
            vmem((others, lanes), jnp.float32),
            smem((others, lanes), jnp.float32),
            smem((far_cap,), jnp.int32),
            smem((far_cap,), jnp.int32),
            pltpu.SemaphoreType.DMA,
        ],
        compiler_params=params(20),
        cost_estimate=cost(100_000_000),
        name="far_density",
    )(counts, wall_flags, remote_live, remote_pairs.T, columns, low, high, far)

    from_above = to_below(back_low)
    from_below = to_above(back_high)
    returned = swap_tiles(back_far, tiles)

    local_sum, own_items = pl.pallas_call(
        functools.partial(local_density_kernel, blocks),
        out_shape=(f32(4, blocks, lanes), i32(own_cap)),
        in_specs=[spec(smem)] * 3 + [spec(vmem)] * 2,
        out_specs=[spec(vmem), spec(smem)],
        scratch_shapes=fields(8) + sums(blocks) + [smem((own_cap,), jnp.int32)],
        compiler_params=params(20),
        cost_estimate=cost(40_000_000),
        name="local_density",
    )(counts, wall_flags, local_pairs.T, table, columns)

    density, picked_density, head_density, tail_density = pl.pallas_call(
        functools.partial(density_kernel, blocks, faces, per_peer),
        out_shape=(f32(blocks, lanes), f32(offered, lanes), f32(faces, lanes), f32(faces, lanes)),
        in_specs=[spec(smem)] + [spec(vmem)] * 7,
        out_specs=[spec(vmem)] * 4,
        name="density",
    )(send_list, table, self_sum, local_sum, far_sum, from_above, from_below, returned)

    low_density = to_above(tail_density)
    high_density = to_below(head_density)
    far_density = swap_tiles(picked_density, tiles)

    force_columns, force_table, pressed, self_force = pl.pallas_call(
        functools.partial(self_force_kernel, blocks),
        out_shape=(columns_shape, f32(blocks * 8, lanes), f32(blocks, lanes), f32(3, blocks, lanes)),
        in_specs=[spec(smem)] + [spec(vmem)] * 2,
        out_specs=[spec(vmem)] * 4,
        scratch_shapes=[stage, vmem((blocks * 8, lanes), jnp.float32)]
        + fields(10)
        + [vmem((blocks * 8, lanes), jnp.float32)],
        compiler_params=params(20),
        cost_estimate=cost(80_000_000),
        name="self_force",
    )(self_items, table, density)

    far_force, force_low, force_high, force_far = pl.pallas_call(
        functools.partial(far_force_kernel, blocks, faces),
        out_shape=(
            f32(3, blocks, lanes),
            f32(faces * 4, lanes),
            f32(faces * 4, lanes),
            f32(offered * 4, lanes),
        ),
        in_specs=[spec(smem)] + [spec(vmem)] * 8,
        out_specs=[spec(vmem)] * 4,
        scratch_shapes=[
            vmem((others * 8, lanes), jnp.float32),
            vmem((others, lanes), jnp.float32),
            vmem((others, lanes), jnp.float32),
        ]
        + fields(10)
        + sums(others),
        compiler_params=params(20),
        cost_estimate=cost(200_000_000),
        name="far_force",
    )(far_items, force_columns, low, high, far, low_density, high_density, far_density, push)

    force_above = to_below(force_low)
    force_below = to_above(force_high)
    force_returned = swap_tiles(force_far, tiles)

    local_force = pl.pallas_call(
        functools.partial(local_force_kernel, blocks),
        out_shape=f32(3, blocks, lanes),
        in_specs=[spec(smem)] + [spec(vmem)] * 3,
        out_specs=spec(vmem),
        scratch_shapes=fields(10) + sums(blocks),
        compiler_params=params(20),
        cost_estimate=cost(80_000_000),
        name="local_force",
    )(own_items, force_columns, force_table, pressed)

    acceleration = pl.pallas_call(
        functools.partial(final_kernel, blocks, faces, per_peer),
        out_shape=f32(3, blocks, lanes),
        in_specs=[spec(smem)] + [spec(vmem)] * 9,
        out_specs=spec(vmem),
        scratch_shapes=[vmem((blocks * 8, lanes), jnp.float32)],
        name="total",
    )(
        send_list,
        table,
        local_sum,
        far_sum,
        self_force,
        local_force,
        far_force,
        force_above,
        force_below,
        force_returned,
    )
    return (density, acceleration)


def solution(mesh):
    placed = (
        P(None, ("slab", "tile"), None),
        P(None, ("slab", "tile"), None),
        P(("slab", "tile"), None),
        P(("slab", "tile"), None),
        P(None, ("slab", "tile"), None),
        P(("slab", "tile")),
        P(("slab", "tile")),
        P(("slab", "tile"), None, None),
        P(("slab", "tile"), None),
        P(("slab", "tile"), None),
        P(("slab", "tile")),
    )
    return jax.shard_map(
        on_device,
        mesh=mesh,
        in_specs=placed,
        out_specs=(P(("slab", "tile"), None), P(None, ("slab", "tile"), None)),
        check_vma=False,
    )
```

profile of v0, /device:TPU:35, one launch (start us, length us, event | category | flops | bytes accessed | tf_op | source)
XLA Modules:
  0.0 157.5 jit_solution(11210195070613136325)
XLA Ops:
  0.6 1.4 copy.14.send
  2.0 2.3 %pack.1 = (f32[512,128]{1,0:T(8,128)}, f32[1024,128]{1,0:T(8,128)}, f32[128,128]{1,0:T(8,128)}, f32[128,128]{1,0:T(8,128)}) custom-call(s32[1,32,4]{2,1,0:T(8,128)} %copy.14.send, f32[3,64,128]{2,1,0:T(8,128)} %pos.1, f32[3,64,128]{2,1,0:T(8,128)} %vel.1, f32[64,128]{1,0:T(8,128)} %mass.1, f32[64,128]{1,0:T(8,128)} %area.1, f32[3,64,128]{2,1,0:T(8,128)} %normal.1, ...), custom_call_target="tpu_custom_call" | custom-call | tf_op jit(solution)/shard_map/pack/pallas_call | solution.py:719
  4.3 10.9 %all-to-all-start = ((f32[32,32,128]{2,1,0:T(8,128)}), f32[32,32,128]{2,1,0:T(8,128)S(1)}, u32[]{:S(2)}, u32[]{:S(2)}) async-start(f32[32,32,128]{2,1,0:T(8,128)} %bitcast.21), calls=%async_computation | async-start | bytes 1048576 | tf_op jit(solution)/shard_map/all_to_all | solution.py:674
  15.2 4.2 %collective-permute-start = (f32[128,128]{1,0:T(8,128)}, f32[128,128]{1,0:T(8,128)S(1)}, u32[]{:S(2)}, u32[]{:S(2)}) collective-permute-start(f32[128,128]{1,0:T(8,128)} %get-tuple-element.33), channel_id=1, source_target_pairs={{0,32},{32,64},{64,96},{96,128},{128,160},{160,192},{192,224},{1,3... | collective-permute-start | bytes 196616 | tf_op jit(solution)/shard_map/ppermute | solution.py:664
  19.5 1.9 %collective-permute-start.1 = (f32[128,128]{1,0:T(8,128)}, f32[128,128]{1,0:T(8,128)S(1)}, u32[]{:S(2)}, u32[]{:S(2)}) collective-permute-start(f32[128,128]{1,0:T(8,128)} %get-tuple-element.34), channel_id=1, source_target_pairs={{32,0},{64,32},{96,64},{128,96},{160,128},{192,160},{224,192},{33,... | collective-permute-start | bytes 196616 | tf_op jit(solution)/shard_map/ppermute | solution.py:669
  22.1 0.9 copy-done
  23.0 0.7 copy-done.13
  23.7 0.7 copy-done.16
  24.3 7.9 %self_density.1 = (bf16[65,128,128]{2,1,0:T(8,128)(2,1)S(1)}, f32[64,128]{1,0:T(8,128)S(1)}, s32[272]{0:T(512)S(1)}) custom-call(s32[64]{0:T(128)S(1)} %copy-done.16, s32[64]{0:T(128)S(1)} %copy-done.13, f32[512,128]{1,0:T(8,128)S(1)} %copy-done), custom_call_target="tpu_custom_call" | custom-call | flops 40000000 | bytes 400000 | tf_op jit(solution)/shard_map/self_density/pallas_call | solution.py:739
  32.2 0.6 copy-done.12
  32.8 0.6 copy-done.22
  33.4 0.0 collective-permute-done.low
  33.4 0.0 collective-permute-done.1.high
  33.4 0.0 all-to-all-done
  33.4 0.0 copy-start.14
  33.4 0.6 copy-done.14
  34.1 0.7 copy-done.17
  34.7 0.7 copy-done.21
  35.4 14.9 %far_density.1 = (f32[4,64,128]{2,1,0:T(8,128)S(1)}, f32[16,128]{1,0:T(8,128)S(1)}, f32[16,128]{1,0:T(8,128)S(1)}, f32[128,128]{1,0:T(8,128)S(1)}, f32[3,160,128]{2,1,0:T(8,128)S(1)}, /*index=5*/s32[656]{0:T(1024)S(1)}) custom-call(s32[64]{0:T(128)S(1)} %copy-done.17, s32[64]{0:T(128)S(1)} %copy-done.14, s32[1]{0:T(128)S(6)} %copy.16.live, ...), custom_call_target="tpu_custom_call" | custom-call | flops 100000000 | bytes 400000 | tf_op jit(solution)/shard_map/far_density/pallas_call | solution.py:750
  50.3 0.6 copy-done.3
  51.0 0.6 copy-done.10
  51.6 0.6 copy-done.19
  52.2 0.6 copy-done.27
  52.8 0.6 copy-done.28
  53.4 17.9 %all-to-all-start.1 = ((f32[32,4,128]{2,1,0:T(4,128)}), f32[32,4,128]{2,1,0:T(4,128)}, u32[]{:S(2)}, u32[]{:S(2)}) async-start(f32[32,4,128]{2,1,0:T(4,128)} %bitcast.15), calls=%async_computation.1 | async-start | bytes 131072 | tf_op jit(solution)/shard_map/all_to_all | solution.py:674
  71.3 1.9 %collective-permute-start.2 = (f32[16,128]{1,0:T(8,128)}, f32[16,128]{1,0:T(8,128)}, u32[]{:S(2)}, u32[]{:S(2)}) collective-permute-start(f32[16,128]{1,0:T(8,128)} %copy-done.28), channel_id=1, source_target_pairs={{32,0},{64,32},{96,64},{128,96},{160,128},{192,160},{224,192},{33,... | collective-permute-start | bytes 24584 | tf_op jit(solution)/shard_map/ppermute | solution.py:669
  73.2 3.6 %collective-permute-start.3 = (f32[16,128]{1,0:T(8,128)}, f32[16,128]{1,0:T(8,128)}, u32[]{:S(2)}, u32[]{:S(2)}) collective-permute-start(f32[16,128]{1,0:T(8,128)} %copy-done.27), channel_id=1, source_target_pairs={{0,32},{32,64},{64,96},{96,128},{128,160},{160,192},{192,224},{1,3... | collective-permute-start | bytes 24584 | tf_op jit(solution)/shard_map/ppermute | solution.py:664
  76.9 0.0 copy-start.15
  76.9 0.6 copy-done.15
  77.5 0.7 copy-done.18
  78.2 0.7 copy-done.26
  78.8 8.7 %local_density.1 = (f32[4,64,128]{2,1,0:T(8,128)S(1)}, s32[272]{0:T(512)S(1)}) custom-call(s32[64]{0:T(128)S(1)} %copy-done.18, s32[64]{0:T(128)S(1)} %copy-done.15, s32[2,64]{1,0:T(2,128)S(1)} %bitcast.19, f32[512,128]{1,0:T(8,128)S(1)} %copy-done.1, bf16[65,128,128]{2,1,0:T(8,128)(2,1)S(1)} %get-tuple-element.31.columns), custom_call_target="tpu_custom_call" | custom-call | flops 40000000 | bytes 400000 | tf_op jit(solution)/shard_map/local_density/pallas_call | solution.py:781
  87.5 0.6 copy-done.4
  88.2 0.6 copy-done.24
  88.8 0.0 collective-permute-done.2.from_above
  88.8 0.0 collective-permute-done.3.from_below
  88.8 0.0 all-to-all-done.1
  88.8 2.4 %density.1 = (f32[64,128]{1,0:T(8,128)}, f32[128,128]{1,0:T(8,128)}, f32[16,128]{1,0:T(8,128)}, f32[16,128]{1,0:T(8,128)}) custom-call(s32[1,32,4]{2,1,0:T(8,128)} %copy.14.send, f32[512,128]{1,0:T(8,128)} %get-tuple-element.29.table, f32[64,128]{1,0:T(8,128)} %copy-done.12, f32[4,64,128]{2,1,0:T(8,128)} %copy-done.4, f32[4,64,128]{2,1,0:T(8,128)} %copy-done.3, ...), custom_call_target="tpu_custom_call" | custom-call | tf_op jit(solution)/shard_map/density/pallas_call | solution.py:792
  91.1 8.3 %all-to-all-start.2 = ((f32[32,4,128]{2,1,0:T(4,128)}), f32[32,4,128]{2,1,0:T(4,128)S(1)}, u32[]{:S(2)}, u32[]{:S(2)}) async-start(f32[32,4,128]{2,1,0:T(4,128)} %bitcast.22), calls=%async_computation.2 | async-start | bytes 131072 | tf_op jit(solution)/shard_map/all_to_all | solution.py:674
  99.5 3.8 %collective-permute-start.4 = (f32[16,128]{1,0:T(8,128)}, f32[16,128]{1,0:T(8,128)S(1)}, u32[]{:S(2)}, u32[]{:S(2)}) collective-permute-start(f32[16,128]{1,0:T(8,128)} %get-tuple-element.48), channel_id=1, source_target_pairs={{0,32},{32,64},{64,96},{96,128},{128,160},{160,192},{192,224},{1,3... | collective-permute-start | bytes 24584 | tf_op jit(solution)/shard_map/ppermute | solution.py:664
  103.3 1.9 %collective-permute-start.5 = (f32[16,128]{1,0:T(8,128)}, f32[16,128]{1,0:T(8,128)S(1)}, u32[]{:S(2)}, u32[]{:S(2)}) collective-permute-start(f32[16,128]{1,0:T(8,128)} %get-tuple-element.49), channel_id=1, source_target_pairs={{32,0},{64,32},{96,64},{128,96},{160,128},{192,160},{224,192},{33,... | collective-permute-start | bytes 24584 | tf_op jit(solution)/shard_map/ppermute | solution.py:669
  105.2 0.0 copy-start.11
  105.2 0.7 copy-done.11
  106.0 0.7 copy-done.23
  106.6 8.4 %self_force.1 = (bf16[65,128,128]{2,1,0:T(8,128)(2,1)S(1)}, f32[512,128]{1,0:T(8,128)S(1)}, f32[64,128]{1,0:T(8,128)S(1)}, f32[3,64,128]{2,1,0:T(8,128)S(1)}) custom-call(s32[272]{0:T(512)S(1)} %copy-done.23, f32[512,128]{1,0:T(8,128)S(1)} %copy-done.2, f32[64,128]{1,0:T(8,128)S(1)} %copy-done.11), custom_call_target="tpu_custom_call" | custom-call | flops 80000000 | bytes 400000 | tf_op jit(solution)/shard_map/self_force/pallas_call | solution.py:804
  115.0 0.7 copy-done.6
  115.7 0.6 copy-done.8
  116.4 0.0 collective-permute-done.4.low_density
  116.4 0.0 collective-permute-done.5.high_density
  116.4 0.0 all-to-all-done.2
  116.4 0.7 copy-done.20
  117.1 8.5 %far_force.1 = (f32[3,64,128]{2,1,0:T(8,128)S(1)}, f32[64,128]{1,0:T(8,128)S(1)}, f32[64,128]{1,0:T(8,128)S(1)}, f32[512,128]{1,0:T(8,128)}) custom-call(s32[656]{0:T(1024)S(1)} %copy-done.20, bf16[65,128,128]{2,1,0:T(8,128)(2,1)S(1)} %get-tuple-element.44.columns, f32[128,128]{1,0:T(8,128)S(1)} %collective-permute-done.low, ...), custom_call_target="tpu_custom_call" | custom-call | flops 200000000 | bytes 400000 | tf_op jit(solution)/shard_map/far_force/pallas_call | solution.py:817
  125.6 0.6 copy-done.9
  126.3 16.4 %all-to-all-start.3 = ((f32[32,16,128]{2,1,0:T(8,128)}), f32[32,16,128]{2,1,0:T(8,128)S(1)}, u32[]{:S(2)}, u32[]{:S(2)}) async-start(f32[32,16,128]{2,1,0:T(8,128)} %bitcast.10), calls=%async_computation.3 | async-start | bytes 524288 | tf_op jit(solution)/shard_map/all_to_all | solution.py:674
  142.7 1.9 %collective-permute-start.6 = (f32[64,128]{1,0:T(8,128)S(1)}, f32[64,128]{1,0:T(8,128)S(1)}, u32[]{:S(2)}, u32[]{:S(2)}) collective-permute-start(f32[64,128]{1,0:T(8,128)S(1)} %get-tuple-element.53), channel_id=1, source_target_pairs={{32,0},{64,32},{96,64},{128,96},{160,128},{192,160},{224,192},{33,... | collective-permute-start | bytes 98312 | tf_op jit(solution)/shard_map/ppermute | solution.py:669
  144.6 3.6 %collective-permute-start.7 = (f32[64,128]{1,0:T(8,128)S(1)}, f32[64,128]{1,0:T(8,128)S(1)}, u32[]{:S(2)}, u32[]{:S(2)}) collective-permute-start(f32[64,128]{1,0:T(8,128)S(1)} %get-tuple-element.54), channel_id=1, source_target_pairs={{0,32},{32,64},{64,96},{96,128},{128,160},{160,192},{192,224},{1,3... | collective-permute-start | bytes 98312 | tf_op jit(solution)/shard_map/ppermute | solution.py:664
  148.3 5.3 %local_force.1 = f32[3,64,128]{2,1,0:T(8,128)S(1)} custom-call(s32[272]{0:T(512)S(1)} %copy-done.25, bf16[65,128,128]{2,1,0:T(8,128)(2,1)S(1)} %get-tuple-element.44.columns, f32[512,128]{1,0:T(8,128)S(1)} %copy-done.7, f32[64,128]{1,0:T(8,128)S(1)} %get-tuple-element.46.pressed), custom_call_target="tpu_custom_call" | custom-call | flops 80000000 | bytes 400000 | tf_op jit(solution)/shard_map/local_force/pallas_call | solution.py:843
  153.6 0.6 copy-done.5
  154.2 0.0 collective-permute-done.6.from_above
  154.3 0.0 all-to-all-done.3
  154.3 0.6 copy-done.30
  154.9 0.0 copy-done.31
  154.9 0.1 copy-done.29
  155.0 2.5 %total.1 = f32[3,64,128]{2,1,0:T(8,128)} custom-call(s32[1,32,4]{2,1,0:T(8,128)} %copy.14.send, f32[512,128]{1,0:T(8,128)} %get-tuple-element.29.table, f32[4,64,128]{2,1,0:T(8,128)} %copy-done.4, f32[4,64,128]{2,1,0:T(8,128)} %copy-done.3, f32[3,64,128]{2,1,0:T(8,128)} %copy-done.8, f32[3,64,128]{2,1,0:T(8,128)} %copy-done.5, f32[3,64,128]{2,1,0:T(8,128)} %copy-done.9, ...), custom_call_target="tpu_custom_call" | custom-call | tf_op jit(solution)/shard_map/total/pallas_call | solution.py:854
  (34 shorter events, 0.1 us)
Async XLA Ops:
  4.3 72.5 %copy-start.1 = (f32[512,128]{1,0:T(8,128)S(1)}, f32[512,128]{1,0:T(8,128)}, u32[]{:S(2)}) copy-start(f32[512,128]{1,0:T(8,128)} %get-tuple-element.29.table) | copy-start | bytes 786436
  4.3 29.1 %all-to-all-start = ((f32[32,32,128]{2,1,0:T(8,128)}), f32[32,32,128]{2,1,0:T(8,128)S(1)}, u32[]{:S(2)}, u32[]{:S(2)}) async-start(f32[32,32,128]{2,1,0:T(8,128)} %bitcast.21), calls=%async_computation | async-start | bytes 1048576 | tf_op jit(solution)/shard_map/all_to_all | solution.py:674
  15.2 18.2 %collective-permute-start = (f32[128,128]{1,0:T(8,128)}, f32[128,128]{1,0:T(8,128)S(1)}, u32[]{:S(2)}, u32[]{:S(2)}) collective-permute-start(f32[128,128]{1,0:T(8,128)} %get-tuple-element.33), channel_id=1, source_target_pairs={{0,32},{32,64},{64,96},{96,128},{128,160},{160,192},{192,224},{1,3... | collective-permute-start | bytes 196616 | tf_op jit(solution)/shard_map/ppermute | solution.py:664
  19.5 13.9 %collective-permute-start.1 = (f32[128,128]{1,0:T(8,128)}, f32[128,128]{1,0:T(8,128)S(1)}, u32[]{:S(2)}, u32[]{:S(2)}) collective-permute-start(f32[128,128]{1,0:T(8,128)} %get-tuple-element.34), channel_id=1, source_target_pairs={{32,0},{64,32},{96,64},{128,96},{160,128},{192,160},{224,192},{33,... | collective-permute-start | bytes 196616 | tf_op jit(solution)/shard_map/ppermute | solution.py:669
  22.1 1.0 copy-start
  23.0 0.7 copy-start.13
  23.7 0.7 copy-start.16
  32.2 0.6 copy-start.12
  32.8 0.6 copy-start.22
  33.4 0.7 copy-start.14
  34.1 0.7 copy-start.17
  34.7 0.7 copy-start.21
  50.3 0.7 copy-start.3
  51.0 0.6 copy-start.10
  51.6 0.6 copy-start.19
  52.2 0.6 copy-start.27
  52.8 0.6 copy-start.28
  53.4 51.8 %copy-start.2 = (f32[512,128]{1,0:T(8,128)S(1)}, f32[512,128]{1,0:T(8,128)}, u32[]{:S(2)}) copy-start(f32[512,128]{1,0:T(8,128)} %get-tuple-element.29.table) | copy-start | bytes 786436
  53.4 35.4 %all-to-all-start.1 = ((f32[32,4,128]{2,1,0:T(4,128)}), f32[32,4,128]{2,1,0:T(4,128)}, u32[]{:S(2)}, u32[]{:S(2)}) async-start(f32[32,4,128]{2,1,0:T(4,128)} %bitcast.15), calls=%async_computation.1 | async-start | bytes 131072 | tf_op jit(solution)/shard_map/all_to_all | solution.py:674
  71.3 17.5 %collective-permute-start.2 = (f32[16,128]{1,0:T(8,128)}, f32[16,128]{1,0:T(8,128)}, u32[]{:S(2)}, u32[]{:S(2)}) collective-permute-start(f32[16,128]{1,0:T(8,128)} %copy-done.28), channel_id=1, source_target_pairs={{32,0},{64,32},{96,64},{128,96},{160,128},{192,160},{224,192},{33,... | collective-permute-start | bytes 24584 | tf_op jit(solution)/shard_map/ppermute | solution.py:669
  73.2 15.6 %collective-permute-start.3 = (f32[16,128]{1,0:T(8,128)}, f32[16,128]{1,0:T(8,128)}, u32[]{:S(2)}, u32[]{:S(2)}) collective-permute-start(f32[16,128]{1,0:T(8,128)} %copy-done.27), channel_id=1, source_target_pairs={{0,32},{32,64},{64,96},{96,128},{128,160},{160,192},{192,224},{1,3... | collective-permute-start | bytes 24584 | tf_op jit(solution)/shard_map/ppermute | solution.py:664
  76.9 0.7 copy-start.15
  77.5 0.7 copy-start.18
  78.2 0.7 copy-start.26
  87.5 0.6 copy-start.4
  88.2 0.6 copy-start.24
  91.1 57.1 %copy-start.25 = (s32[272]{0:T(512)S(1)}, s32[272]{0:T(512)}, u32[]{:S(2)}) copy-start(s32[272]{0:T(512)} %copy-done.24) | copy-start | bytes 3268
  91.1 25.2 %all-to-all-start.2 = ((f32[32,4,128]{2,1,0:T(4,128)}), f32[32,4,128]{2,1,0:T(4,128)S(1)}, u32[]{:S(2)}, u32[]{:S(2)}) async-start(f32[32,4,128]{2,1,0:T(4,128)} %bitcast.22), calls=%async_computation.2 | async-start | bytes 131072 | tf_op jit(solution)/shard_map/all_to_all | solution.py:674
  99.5 16.9 %collective-permute-start.4 = (f32[16,128]{1,0:T(8,128)}, f32[16,128]{1,0:T(8,128)S(1)}, u32[]{:S(2)}, u32[]{:S(2)}) collective-permute-start(f32[16,128]{1,0:T(8,128)} %get-tuple-element.48), channel_id=1, source_target_pairs={{0,32},{32,64},{64,96},{96,128},{128,160},{160,192},{192,224},{1,3... | collective-permute-start | bytes 24584 | tf_op jit(solution)/shard_map/ppermute | solution.py:664
  103.3 13.1 %collective-permute-start.5 = (f32[16,128]{1,0:T(8,128)}, f32[16,128]{1,0:T(8,128)S(1)}, u32[]{:S(2)}, u32[]{:S(2)}) collective-permute-start(f32[16,128]{1,0:T(8,128)} %get-tuple-element.49), channel_id=1, source_target_pairs={{32,0},{64,32},{96,64},{128,96},{160,128},{192,160},{224,192},{33,... | collective-permute-start | bytes 24584 | tf_op jit(solution)/shard_map/ppermute | solution.py:669
  105.2 0.8 copy-start.11
  106.0 0.7 copy-start.23
  115.0 0.7 copy-start.6
  115.7 0.6 copy-start.8
  116.4 31.9 %copy-start.7 = (f32[512,128]{1,0:T(8,128)S(1)}, f32[512,128]{1,0:T(8,128)}, u32[]{:S(2)}) copy-start(f32[512,128]{1,0:T(8,128)} %copy-done.6) | copy-start | bytes 786436
  116.4 0.7 copy-start.20
  125.6 0.6 copy-start.9
  126.3 28.0 %all-to-all-start.3 = ((f32[32,16,128]{2,1,0:T(8,128)}), f32[32,16,128]{2,1,0:T(8,128)S(1)}, u32[]{:S(2)}, u32[]{:S(2)}) async-start(f32[32,16,128]{2,1,0:T(8,128)} %bitcast.10), calls=%async_computation.3 | async-start | bytes 524288 | tf_op jit(solution)/shard_map/all_to_all | solution.py:674
  142.7 11.6 %collective-permute-start.6 = (f32[64,128]{1,0:T(8,128)S(1)}, f32[64,128]{1,0:T(8,128)S(1)}, u32[]{:S(2)}, u32[]{:S(2)}) collective-permute-start(f32[64,128]{1,0:T(8,128)S(1)} %get-tuple-element.53), channel_id=1, source_target_pairs={{32,0},{64,32},{96,64},{128,96},{160,128},{192,160},{224,192},{33,... | collective-permute-start | bytes 98312 | tf_op jit(solution)/shard_map/ppermute | solution.py:669
  144.6 9.6 %collective-permute-start.7 = (f32[64,128]{1,0:T(8,128)S(1)}, f32[64,128]{1,0:T(8,128)S(1)}, u32[]{:S(2)}, u32[]{:S(2)}) collective-permute-start(f32[64,128]{1,0:T(8,128)S(1)} %get-tuple-element.54), channel_id=1, source_target_pairs={{0,32},{32,64},{64,96},{96,128},{128,160},{160,192},{192,224},{1,3... | collective-permute-start | bytes 98312 | tf_op jit(solution)/shard_map/ppermute | solution.py:664
  153.6 0.6 copy-start.5
  154.2 0.6 copy-start.30
  154.3 0.6 copy-start.31
  154.3 0.7 copy-start.29
where the time goes:
time: 160 us; the launch traced here: 158 us
  starting transfers between devices  76.5 us (48%)
  Pallas kernels  60.9 us (38%)
  local copies, waits for them, and re-layouts  18.5 us (12%)
    all_to_all x4, starting transfers between devices, swap_tiles(): lax.all_to_all(parts, 'tile', split_axis=0, concat_axis=0, tiled=True)  53.5 us
    unnamed x65, local copies, waits for them, and re-layouts  18.5 us
    ppermute x4, starting transfers between devices, to_above(): return lax.ppermute(shard, 'slab', [(i, i + 1) for i in range(count - 1)])  15.3 us
    pallas_call x1, Pallas kernels, on_device(): pl.pallas_call(functools.partial(far_density_kernel, blocks, faces), out_...  14.9 us
    pallas_call x1, Pallas kernels, on_device(): pl.pallas_call(functools.partial(local_density_kernel, blocks), out_shape...  8.66 us
    pallas_call x1, Pallas kernels, on_device(): pl.pallas_call(functools.partial(far_force_kernel, blocks, faces), out_sh...  8.51 us
    pallas_call x1, Pallas kernels, on_device(): pl.pallas_call(functools.partial(self_force_kernel, blocks), out_shape=(c...  8.39 us
    pallas_call x1, Pallas kernels, on_device(): pl.pallas_call(functools.partial(self_density_kernel, blocks), out_shape=...  7.87 us
  transfers between devices with their start and end apart: 12, of which 0 were waited for; matrix products, arithmetic and copies ran while one was open for 0% of the time, Pallas kernels for 19%

commit v1 on v0

v1 whole, which is shorter than its diff:
```python
import functools
import math

import jax
import jax.numpy as jnp
from jax import lax
from jax.experimental import pallas as pl
from jax.experimental.pallas import tpu as pltpu
from jax.sharding import PartitionSpec as P

kernel_norm = 21.0 / (16.0 * math.pi)
softening = 0.01
tiny = 1e-30
lanes = 128
rows_item = 32
groups = rows_item // 8
batch = lanes // rows_item
halves = 2
pair_pad = 8
bf16 = jnp.bfloat16
vmem = pltpu.VMEM
smem = pltpu.SMEM


def spec(space):
    return pl.BlockSpec(memory_space=space)


def params(mib):
    return pltpu.CompilerParams(vmem_limit_bytes=mib * 1024 * 1024)


def column_of(row):
    number = row.shape[1]
    same = lax.broadcasted_iota(jnp.int32, (number, number), 0) == lax.broadcasted_iota(
        jnp.int32, (number, number), 1
    )
    return jnp.sum(jnp.where(same, row, 0.0), axis=1, keepdims=True)


def pack_kernel(
    blocks, faces, per_peer, send, pos, vel, mass, area, normal, flags_row, counts_row, table, picked, head, tail
):
    slot = lax.broadcasted_iota(jnp.int32, (blocks, lanes), 1).astype(jnp.float32)
    alive = slot < column_of(counts_row[...].astype(jnp.float32))
    wall_value = column_of(flags_row[...].astype(jnp.float32)) + jnp.zeros((blocks, lanes), jnp.float32)
    wall = wall_value > 0.5
    nx, ny, nz = normal[0], normal[1], normal[2]
    length = jnp.sqrt(nx * nx + ny * ny + nz * nz)
    weight = jnp.where(alive, jnp.where(wall, area[...], mass[...]), 0.0)
    wall_scale = weight / length
    parts = (nx, ny, nz)
    for c in range(3):
        table[pl.ds(c, blocks, stride=8), :] = 0.5 * pos[c]
        table[pl.ds(3 + c, blocks, stride=8), :] = jnp.where(wall, wall_scale * parts[c], vel[c])
    table[pl.ds(6, blocks, stride=8), :] = weight
    table[pl.ds(7, blocks, stride=8), :] = wall_value
    head[...] = table[0 : faces * 8, :]
    tail[...] = table[(blocks - faces) * 8 : blocks * 8, :]

    def pick(t, carry):
        for k in range(per_peer):
            source = pl.multiple_of(send[0, t, k] * 8, 8)
            at = pl.multiple_of((t * per_peer + k) * 8, 8)
            picked[pl.ds(at, 8), :] = table[pl.ds(source, 8), :]
        return carry

    lax.fori_loop(0, picked.shape[0] // (8 * per_peer), pick, 0, unroll=2)


def rounded(x):
    return x.astype(bf16).astype(jnp.float32)


def split3(x):
    high = rounded(x)
    rest = x - high
    middle = rounded(rest)
    return high, middle, rest - middle


def make_spread(spread):
    shape = spread.shape
    k = lax.broadcasted_iota(jnp.int32, shape, 0) & 31
    tile = lax.broadcasted_iota(jnp.int32, shape, 1) >> 7
    want = jnp.where(tile == 3, 6, jnp.where(tile > 3, tile - 1, tile))
    want = jnp.where(tile == 7, 7, want)
    hit = jnp.logical_and(jnp.logical_and(k < 24, (k & 7) == want), tile < 8)
    hit = jnp.logical_or(hit, jnp.logical_and(jnp.logical_and(k >= 24, k < 27), tile == 8))
    spread[...] = jnp.where(hit, 1.0, 0.0).astype(bf16)


def make_columns(blocks, table, last, columns, stage):
    lane = lax.broadcasted_iota(jnp.int32, (lanes, lanes), 1) >> 5
    for g in range(blocks // 4):
        for j in range(4):
            b = 4 * g + j
            for p, piece in enumerate(split3(table[8 * b : 8 * b + 8, :])):
                stage[32 * b + 8 * p : 32 * b + 8 * p + 8, :] = piece
            if last is None:
                stage[32 * b + 24 : 32 * b + 32, :] = jnp.zeros((8, lanes), jnp.float32)
            else:
                stage[32 * b + 24 : 32 * b + 32, :] = last[8 * b : 8 * b + 8, :]

    def some(g, carry):
        turned = stage[pl.ds(pl.multiple_of(g * lanes, lanes), lanes), :].T
        for j in range(4):
            columns[g * 4 + j] = jnp.where(lane == j, turned, 0.0).astype(bf16)
        return carry

    lax.fori_loop(0, blocks // 4, some, 0)
    columns[blocks] = jnp.zeros((lanes, lanes), bf16)


def put_items(items, at, code):
    for k in range(lanes // rows_item):
        items[at + k] = code | (k << 16)


def close_items(items, count, blocks):
    for k in range(2 * batch * halves):
        items[count + k] = jnp.int32(blocks)


def chunks(count):
    return (count + (rows_item - 1)) >> 5


def decode(code):
    first = code & 255
    second = (code >> 8) & 255
    row = pl.multiple_of((code >> 16) * rows_item, rows_item)
    return first, second, row


def wide(row):
    return jnp.broadcast_to(row, (8, lanes))


def spread_fields(columns, spread, wide_fields, tiles, decoded):
    left = jnp.concatenate([columns[first, pl.ds(row, rows_item), :] for first, second, row in decoded], axis=0)
    for t in range((tiles + 1) // 2):
        both = jnp.dot(left, spread[:, 256 * t : 256 * t + 256], preferred_element_type=jnp.float32)
        wide_fields[2 * t] = both[:, 0:lanes]
        wide_fields[2 * t + 1] = both[:, lanes : 2 * lanes]


def close_u(fields, rows):
    dx = fields[0] - rows[0]
    dy = fields[1] - rows[1]
    dz = fields[2] - rows[2]
    square = dx * dx + dy * dy + dz * dz
    safe = jnp.maximum(square, tiny)
    q = safe * lax.rsqrt(safe)
    u = jnp.maximum(1.0 - q, 0.0)
    return dx, dy, dz, square, u


def kernel_shape(u):
    u2 = u * u
    return (u2 * u2) * (5.0 - 4.0 * u)


def run_items(columns, spread, wide_fields, tiles, items, start, count, body, finish):
    def parts(it):
        for h in range(halves):
            yield h, [decode(items[start + (it * halves + h) * batch + k]) for k in range(batch)]

    def prepare(it):
        for h, decoded in parts(it):
            spread_fields(columns, spread, wide_fields[h], tiles, decoded)

    def step(it, carry):
        done = [(decoded, body(wide_fields[h], decoded)) for h, decoded in parts(it)]
        prepare(it + 1)
        for decoded, outs in done:
            finish(decoded, outs)
        return carry

    prepare(0)
    size = batch * halves
    lax.fori_loop(0, (count + size - 1) >> 3, step, 0)


def merge_lanes(values, first, lane):
    base = (first & 15) * 8
    total = jnp.zeros((8, lanes), jnp.float32)
    for c, value in enumerate(values):
        total = jnp.where(lane == base + c, value, total)
    return total


def merge_rows(values, sub, places):
    total = jnp.zeros((8, lanes), jnp.float32)
    for c, value in zip(places, values):
        total = jnp.where(sub == c, jnp.sum(value, axis=0, keepdims=True), total)
    return total


def add_sums(acc_first, acc_second, decoded, outs):
    for (first, second, row), (merged, tile) in zip(decoded, outs):
        if merged:
            slab = first >> 4
            for g in range(groups):
                acc_first[slab, pl.ds(row + 8 * g, 8), :] += merged[g]
        if tile is not None:
            at = pl.multiple_of(second * 8, 8)
            acc_second[pl.ds(at, 8), :] += tile


def density_body(source, kind, wide_fields, decoded):
    lane = lax.broadcasted_iota(jnp.int32, (8, lanes), 1)
    sub = lax.broadcasted_iota(jnp.int32, (8, lanes), 0)
    places = {"self": (0,), "local": (0,), "both": (0, 1, 2, 3), "second": (0, 4, 5, 6)}
    outs = []
    for k, (first, second, row) in enumerate(decoded):
        base = pl.multiple_of(second * 8, 8)
        rows = [wide(source[pl.ds(base + c, 1), :]) for c in range(3)]
        given = []
        if kind in ("both", "local", "first"):
            given = [wide(source[pl.ds(base + 6, 1), :])]
            if kind == "first":
                given += [wide(source[pl.ds(base + 3 + c, 1), :]) for c in range(3)]
        merged = []
        sums = None
        for g in range(groups):
            at = rows_item * k + 8 * g
            number = {"first": 3, "second": 7}.get(kind, 4)
            fields = [wide_fields[f, at : at + 8, :] for f in range(number)]
            dx, dy, dz, square, u = close_u(fields, rows)
            w = kernel_shape(u)
            if given:
                values = [jnp.sum(w * other, axis=1, keepdims=True) for other in given]
                merged.append(merge_lanes(values, first, lane))
            if kind != "first":
                back = [w * field for field in fields[3:]]
                if kind == "both":
                    slope = ((u * u) * u) * fields[3]
                    back += [slope * d for d in (dx, dy, dz)]
                sums = back if sums is None else [s + b for s, b in zip(sums, back)]
        outs.append((merged, merge_rows(sums, sub, places[kind]) if sums else None))
    return outs


def clear(ref, pieces):
    size = ref.shape[0] // pieces

    def some(k, carry):
        at = pl.multiple_of(k * size, size)
        ref[pl.ds(at, size)] = jnp.zeros((size,) + tuple(ref.shape[1:]), jnp.float32)
        return carry

    lax.fori_loop(0, pieces, some, 0)


def plane(ref, number, c):
    return ref[pl.ds(c, number, stride=8), :]


def first_rows(acc_first, turned, blocks):
    for s in range(blocks // 16):
        turned[s * lanes : (s + 1) * lanes, :] = acc_first[s].T


def run_density(columns, spread, fields, source, acc_first, acc_second, kind, items, start, count):
    run_items(
        columns,
        spread,
        fields,
        7 if kind == "second" else 4,
        items,
        start,
        count,
        functools.partial(density_body, source, kind),
        functools.partial(add_sums, acc_first, acc_second),
    )


def self_density_kernel(
    blocks,
    counts,
    flags,
    live,
    local_pairs,
    remote_pairs,
    table,
    columns,
    own,
    items,
    local_items,
    far_pairs,
    stage,
    spread,
    wide_a,
    wide_b,
    acc_second,
):
    make_columns(blocks, table, None, columns, stage)
    make_spread(spread)
    clear(acc_second, 4)
    zero = jnp.int32(0)

    def self_step(b, n):
        put_items(items, n, b | (b << 8))
        return n + chunks(counts[b]) * (1 - flags[b])

    count = lax.fori_loop(0, blocks, self_step, zero, unroll=8)
    close_items(items, count, blocks)
    items[items.shape[0] - 1] = count
    run_density(columns, spread, (wide_a, wide_b), table, None, acc_second, "self", items, 0, count)
    own[...] = plane(acc_second, blocks, 0)
    cap = local_items.shape[0] // 2

    def local_step(p, state):
        n_both, n_wall = state
        a = local_pairs[0, p]
        b = local_pairs[1, p]
        wall_b = flags[b]
        kinds = flags[a] + wall_b
        swap = jnp.where(kinds == 1, wall_b, (counts[b] < counts[a]).astype(jnp.int32)) > 0
        first = jnp.where(swap, b, a)
        second = jnp.where(swap, a, b)
        number = chunks(counts[first])
        put_items(local_items, jnp.where(kinds == 0, n_both, n_wall), first | (second << 8))
        return n_both + jnp.where(kinds == 0, number, 0), n_wall + jnp.where(kinds == 1, number, 0)

    n_both, n_wall = lax.fori_loop(0, local_pairs.shape[1], local_step, (zero, zero + cap), unroll=8)
    close_items(local_items, n_both, blocks)
    close_items(local_items, n_wall, blocks)
    local_items[cap - 1] = n_both
    local_items[2 * cap - 1] = n_wall - cap
    half = far_pairs.shape[0] // 2

    def remote_step(p, state):
        n_fluid, n_wall = state
        a = remote_pairs[0, p]
        j = remote_pairs[1, p]
        b = jnp.where(j < blocks, j, j - blocks)
        wall = flags[a]
        code = a | (b << 8) | (chunks(counts[a]) << 16)
        far_pairs[jnp.where(wall > 0, n_wall, n_fluid)] = code
        return n_fluid + 1 - wall, n_wall + wall

    n_fluid, n_wall = lax.fori_loop(0, live[0], remote_step, (zero, zero + half))
    far_pairs[half - 1] = n_fluid
    far_pairs[2 * half - 1] = n_wall - half
    for k in range(pair_pad):
        far_pairs[n_fluid + k] = zero
        far_pairs[n_wall + k] = zero


def local_density_kernel(
    blocks,
    items,
    table,
    columns,
    own,
    spread,
    wide_a,
    wide_b,
    acc_first,
    acc_second,
    turned,
):
    make_spread(spread)
    clear(acc_first, 1)
    clear(acc_second, 4)
    density = functools.partial(run_density, columns, spread, (wide_a, wide_b), table, acc_first, acc_second)
    cap = items.shape[0] // 2
    density("local", items, 0, items[cap - 1])
    density("second", items, cap, items[2 * cap - 1])
    first_rows(acc_first, turned, blocks)
    own[0] = plane(turned, blocks, 0) + plane(acc_second, blocks, 0)
    for c in range(1, 4):
        own[c] = plane(acc_second, blocks, 3 + c)


def rows_out(tiles, out, start, number):
    for k in range(number):
        out[4 * k : 4 * k + 4, :] = tiles[8 * (start + k) : 8 * (start + k) + 4, :]


def far_density_kernel(
    blocks,
    faces,
    far_pairs,
    columns,
    low,
    high,
    far,
    own,
    back_low,
    back_high,
    back_far,
    push,
    items,
    spread,
    wide_a,
    wide_b,
    acc_first,
    acc_second,
    turned,
    source,
    wall_rows,
    wall_flag,
    wall_items,
    sem,
):
    others = source.shape[0] // 8
    source[0 : faces * 8, :] = low[...]
    source[faces * 8 : 2 * faces * 8, :] = high[...]
    source[2 * faces * 8 :, :] = far[...]
    wall_rows[...] = plane(source, others, 7)
    copy = pltpu.make_async_copy(wall_rows, wall_flag, sem)
    copy.start()
    make_spread(spread)
    clear(acc_first, 1)
    clear(acc_second, 4)
    copy.wait()
    zero = jnp.int32(0)
    half = far_pairs.shape[0] // 2
    cap = items.shape[0] // 2

    def fluid_second(code):
        return wall_flag[(code >> 8) & 255, 0] < 0.5

    def wall_step(q, n):
        for k in range(pair_pad):
            code = far_pairs[half + q * pair_pad + k]
            put_items(wall_items, n, code & 65535)
            n = n + jnp.where(fluid_second(code), code >> 16, 0)
        return n

    def fluid_step(q, state):
        n_both, n_first = state
        for k in range(pair_pad):
            code = far_pairs[q * pair_pad + k]
            number = code >> 16
            fluid = fluid_second(code)
            put_items(items, jnp.where(fluid, n_both, n_first), code & 65535)
            n_both = n_both + jnp.where(fluid, number, 0)
            n_first = n_first + jnp.where(fluid, 0, number)
        return n_both, n_first

    def passes(pairs):
        return (pairs + (pair_pad - 1)) >> 3

    n_both, n_first = lax.fori_loop(0, passes(far_pairs[half - 1]), fluid_step, (zero, zero + cap))
    close_items(items, n_both, blocks)
    close_items(items, n_first, blocks)
    items[cap - 1] = n_both
    n_second = lax.fori_loop(0, passes(far_pairs[2 * half - 1]), wall_step, zero)
    close_items(wall_items, n_second, blocks)
    density = functools.partial(run_density, columns, spread, (wide_a, wide_b), source, acc_first, acc_second)
    density("second", wall_items, 0, n_second)
    density("both", items, 0, n_both)
    density("first", items, cap, n_first - cap)
    first_rows(acc_first, turned, blocks)
    for c in range(4):
        own[c] = plane(turned, blocks, c)
    rows_out(acc_second, back_low, 0, faces)
    rows_out(acc_second, back_high, faces, faces)
    rows_out(acc_second, back_far, 2 * faces, others - 2 * faces)
    for c in range(3):
        push[c] = plane(acc_second, others, 4 + c)


def fluid_mask(blocks, table):
    return jnp.logical_and(plane(table, blocks, 6) > 0.0, plane(table, blocks, 7) < 0.5)


def density_kernel(
    blocks,
    faces,
    per_peer,
    send,
    table,
    self_sum,
    local_sum,
    far_sum,
    from_above,
    from_below,
    returned,
    density,
    slopes,
    total,
):
    total[pl.ds(0, blocks, stride=8), :] = self_sum[...] + local_sum[0] + far_sum[0]
    for c in range(1, 8):
        total[pl.ds(c, blocks, stride=8), :] = jnp.zeros((blocks, lanes), jnp.float32)
    for k in range(faces):
        at = 8 * (blocks - faces + k)
        total[at : at + 4, :] += from_above[4 * k : 4 * k + 4, :]
        total[8 * k : 8 * k + 4, :] += from_below[4 * k : 4 * k + 4, :]

    def give(t, carry):
        for k in range(per_peer):
            at = pl.multiple_of(send[0, t, k] * 8, 8)
            source = pl.multiple_of((t * per_peer + k) * 4, 4)
            total[pl.ds(at, 4), :] += returned[pl.ds(source, 4), :]
        return carry

    lax.fori_loop(0, send.shape[1], give, 0, unroll=2)
    density[...] = jnp.where(fluid_mask(blocks, table), kernel_norm * plane(total, blocks, 0), 0.0)
    for c in range(3):
        slopes[c] = plane(total, blocks, 1 + c)


def force_fields(source, density, number, pressed):
    mass = plane(source, number, 6)
    rho = jnp.where(mass > 0.0, density, 1.0)
    inverse = 1.0 / jnp.where(rho > 0.0, rho, 1.0)
    scaled = mass * inverse
    source[pl.ds(7, number, stride=8), :] = scaled
    press = 10.0 * (rho - 1.0) * inverse * scaled
    pressed[...] = press
    return press


def force_body(source, pressed, kind, wide_fields, decoded):
    lane = lax.broadcasted_iota(jnp.int32, (8, lanes), 1)
    sub = lax.broadcasted_iota(jnp.int32, (8, lanes), 0)
    outs = []
    for k, (first, second, row) in enumerate(decoded):
        base = pl.multiple_of(second * 8, 8)
        rows = [wide(source[pl.ds(base + c, 1), :]) for c in range(6 if kind == "second" else 8)]
        if kind != "second":
            press = wide(pressed[pl.ds(second, 1), :])
        merged = []
        sums = None
        for g in range(groups):
            at = rows_item * k + 8 * g
            fields = [wide_fields[f, at : at + 8, :] for f in range(9)]
            dx, dy, dz, square, u = close_u(fields, rows)
            u3 = (u * u) * u
            damp = u3 * (square * (1.0 / (square + 0.25 * softening)))
            if kind == "second":
                damp = damp * fields[7]
                pull = u3 * fields[8]
                values = [damp * (fields[4 + c] - rows[3 + c]) for c in range(3)]
                values += [pull * d for d in (dx, dy, dz)]
            else:
                damp = damp * (fields[7] * rows[7])
                pull = u3 * (fields[8] * rows[6] + fields[3] * press)
                values = [
                    pull * d - damp * (fields[4 + c] - rows[3 + c]) for c, d in enumerate((dx, dy, dz))
                ]
            if kind in ("local", "first"):
                merged.append(
                    merge_lanes([jnp.sum(v, axis=1, keepdims=True) for v in values], first, lane)
                )
            if kind != "first":
                sums = values if sums is None else [s + v for s, v in zip(sums, values)]
        outs.append((merged, merge_rows(sums, sub, range(1, 7)) if sums else None))
    return outs


def run_force(columns, spread, fields, source, pressed, acc_first, acc_second, kind, items, cap):
    run_items(
        columns,
        spread,
        fields,
        9,
        items,
        0,
        items[cap - 1],
        functools.partial(force_body, source, pressed, kind),
        functools.partial(add_sums, acc_first, acc_second),
    )


def far_send_kernel(
    blocks,
    faces,
    per_peer,
    send,
    items,
    table,
    density,
    low,
    high,
    far,
    push,
    columns,
    own_source,
    pressed,
    out_low,
    out_high,
    out_far,
    stage,
    last,
    source,
    spread,
    wide_a,
    wide_b,
    acc_second,
):
    others = source.shape[0] // 8
    source[0 : faces * 8, :] = low[...]
    source[faces * 8 : 2 * faces * 8, :] = high[...]
    source[2 * faces * 8 :, :] = far[...]
    own_source[...] = table[...]
    press = force_fields(own_source, density[...], blocks, pressed)
    last[...] = jnp.zeros(last.shape, jnp.float32)
    for p, piece in enumerate(split3(press)):
        last[pl.ds(p, blocks, stride=8), :] = piece
    make_columns(blocks, own_source, last, columns, stage)
    make_spread(spread)
    clear(acc_second, 4)
    run_force(columns, spread, (wide_a, wide_b), source, None, None, acc_second, "second", items, items.shape[0] // 2)
    for c in range(3):
        acc_second[pl.ds(4 + c, others, stride=8), :] = push[c] - plane(acc_second, others, 4 + c)
    acc_second[pl.ds(0, faces, stride=8), :] = density[0:faces, :]
    acc_second[pl.ds(8 * faces, faces, stride=8), :] = density[blocks - faces :, :]

    def pick(t, carry):
        for k in range(per_peer):
            at = 8 * (2 * faces + t * per_peer + k)
            acc_second[pl.ds(at, 1), :] = density[pl.ds(send[0, t, k], 1), :]
        return carry

    lax.fori_loop(0, send.shape[1], pick, 0, unroll=4)
    out_low[...] = acc_second[0 : 8 * faces, :]
    out_high[...] = acc_second[8 * faces : 16 * faces, :]
    out_far[...] = acc_second[16 * faces :, :]


def own_force_kernel(
    blocks,
    self_items,
    both_items,
    columns,
    source,
    pressed,
    own,
    spread,
    wide_a,
    wide_b,
    acc_first,
    acc_second,
    turned,
):
    make_spread(spread)
    clear(acc_first, 1)
    clear(acc_second, 4)
    force = functools.partial(
        run_force, columns, spread, (wide_a, wide_b), source, pressed, acc_first, acc_second
    )
    force("self", self_items, self_items.shape[0])
    force("local", both_items, both_items.shape[0] // 2)
    first_rows(acc_first, turned, blocks)
    for c in range(3):
        own[c] = plane(turned, blocks, c) - plane(acc_second, blocks, 1 + c)


def far_force_kernel(
    blocks,
    faces,
    items,
    columns,
    low,
    high,
    far,
    from_below,
    from_above,
    returned,
    own,
    source,
    source_density,
    pressed,
    spread,
    wide_a,
    wide_b,
    acc_first,
    turned,
):
    others = source.shape[0] // 8
    source[0 : faces * 8, :] = low[...]
    source[faces * 8 : 2 * faces * 8, :] = high[...]
    source[2 * faces * 8 :, :] = far[...]
    source_density[0:faces, :] = plane(from_below, faces, 0)
    source_density[faces : 2 * faces, :] = plane(from_above, faces, 0)
    source_density[2 * faces :, :] = plane(returned, others - 2 * faces, 0)
    force_fields(source, source_density[...], others, pressed)
    make_spread(spread)
    clear(acc_first, 1)
    run_force(columns, spread, (wide_a, wide_b), source, pressed, acc_first, None, "first", items, items.shape[0] // 2)
    first_rows(acc_first, turned, blocks)
    for c in range(3):
        own[c] = plane(turned, blocks, c)


def final_kernel(
    blocks,
    faces,
    per_peer,
    send,
    table,
    density,
    slopes,
    local_sum,
    far_sum,
    own_force,
    far_force,
    from_above,
    from_below,
    returned,
    out,
    total,
):
    total[...] = jnp.zeros(total.shape, jnp.float32)
    total[8 * (blocks - faces) :, :] += from_above[...]
    total[0 : 8 * faces, :] += from_below[...]

    def give(t, carry):
        for k in range(per_peer):
            at = pl.multiple_of(send[0, t, k] * 8, 8)
            source = pl.multiple_of((t * per_peer + k) * 8, 8)
            total[pl.ds(at, 8), :] += returned[pl.ds(source, 8), :]
        return carry

    lax.fori_loop(0, send.shape[1], give, 0, unroll=2)
    fluid = fluid_mask(blocks, table)
    mass = plane(table, blocks, 6)
    over_mass = 1.0 / jnp.where(mass > 0.0, mass, 1.0)
    over_rho = 1.0 / jnp.where(fluid, density[...], 1.0)
    press = jnp.where(fluid, 10.0 * (density[...] - 1.0) * over_rho * over_rho, 0.0)
    for c in range(3):
        force = (own_force[c] + far_force[c]) * over_mass
        force = force + local_sum[1 + c] + far_sum[1 + c]
        force = force + plane(total, blocks, 1 + c) * over_rho + plane(total, blocks, 4 + c)
        out[c] = jnp.where(fluid, kernel_norm * (force - press * slopes[c]), 0.0)


def f32(*shape):
    return jax.ShapeDtypeStruct(shape, jnp.float32)


def i32(*shape):
    return jax.ShapeDtypeStruct(shape, jnp.int32)


def to_above(shard):
    count = lax.axis_size("slab")
    return lax.ppermute(shard, "slab", [(i, i + 1) for i in range(count - 1)])


def to_below(shard):
    count = lax.axis_size("slab")
    return lax.ppermute(shard, "slab", [(i + 1, i) for i in range(count - 1)])


def swap_tiles(rows, tiles):
    parts = rows.reshape(tiles, rows.shape[0] // tiles, lanes)
    return lax.all_to_all(parts, "tile", split_axis=0, concat_axis=0, tiled=True).reshape(rows.shape)


def on_device(
    positions,
    velocities,
    masses,
    wall_areas,
    normals,
    wall_flags,
    counts,
    send_list,
    local_pairs,
    remote_pairs,
    remote_live,
):
    blocks = positions.shape[1]
    faces = blocks // 4
    tiles = lax.axis_size("tile")
    per_peer = send_list.shape[2]
    offered = send_list.shape[1] * per_peer
    others = 2 * faces + offered
    n_local = local_pairs.shape[0]
    n_remote = remote_pairs.shape[0]
    per = lanes // rows_item
    spare = 3 * batch * halves
    self_cap = per * blocks + spare
    own_cap = per * n_local + spare
    far_cap = per * n_remote + spare
    pair_cap = n_remote + 2 * pair_pad
    columns_shape = jax.ShapeDtypeStruct((blocks + 1, lanes, lanes), bf16)
    stage = vmem((blocks * 32, lanes), jnp.float32)

    def fields(number):
        return [vmem((lanes, 128 * number), bf16)] + [vmem((number, lanes, lanes), jnp.float32)] * 2

    acc_first = vmem((blocks // 16 + 1, lanes, lanes), jnp.float32)
    turned = vmem((blocks * 8, lanes), jnp.float32)

    def tiles_of(number):
        return vmem((number * 8, lanes), jnp.float32)

    def cost(flops):
        return pl.CostEstimate(flops=flops, bytes_accessed=400_000, transcendentals=0)

    table, picked, head, tail = pl.pallas_call(
        functools.partial(pack_kernel, blocks, faces, per_peer),
        out_shape=(f32(blocks * 8, lanes), f32(offered * 8, lanes), f32(faces * 8, lanes), f32(faces * 8, lanes)),
        in_specs=[spec(smem)] + [spec(vmem)] * 7,
        out_specs=[spec(vmem)] * 4,
        compiler_params=params(8),
        name="pack",
    )(
        send_list,
        positions,
        velocities,
        masses,
        wall_areas,
        normals,
        wall_flags[None, :],
        counts[None, :],
    )
    low = to_above(tail)
    high = to_below(head)
    far = swap_tiles(picked, tiles)

    columns, self_sum, self_items, own_items, far_pairs = pl.pallas_call(
        functools.partial(self_density_kernel, blocks),
        out_shape=(
            columns_shape,
            f32(blocks, lanes),
            i32(self_cap),
            i32(2 * own_cap),
            i32(2 * pair_cap),
        ),
        in_specs=[spec(smem)] * 5 + [spec(vmem)],
        out_specs=[spec(vmem)] * 2 + [spec(smem)] * 3,
        scratch_shapes=[stage] + fields(8) + [tiles_of(blocks)],
        compiler_params=params(12),
        cost_estimate=cost(40_000_000),
        name="self_density",
    )(counts, wall_flags, remote_live, local_pairs.T, remote_pairs.T, table)

    far_sum, back_low, back_high, back_far, push, far_items = pl.pallas_call(
        functools.partial(far_density_kernel, blocks, faces),
        out_shape=(
            f32(4, blocks, lanes),
            f32(faces * 4, lanes),
            f32(faces * 4, lanes),
            f32(offered * 4, lanes),
            f32(3, others, lanes),
            i32(2 * far_cap),
        ),
        in_specs=[spec(smem)] + [spec(vmem)] * 4,
        out_specs=[spec(vmem)] * 5 + [spec(smem)],
        scratch_shapes=fields(8)
        + [acc_first, tiles_of(others), turned]
        + [
            tiles_of(others),
            vmem((others, lanes), jnp.float32),
            smem((others, lanes), jnp.float32),
            smem((far_cap,), jnp.int32),
            pltpu.SemaphoreType.DMA,
        ],
        compiler_params=params(12),
        cost_estimate=cost(100_000_000),
        name="far_density",
    )(far_pairs, columns, low, high, far)

    from_above = to_below(back_low)
    from_below = to_above(back_high)
    returned = swap_tiles(back_far, tiles)

    local_sum = pl.pallas_call(
        functools.partial(local_density_kernel, blocks),
        out_shape=f32(4, blocks, lanes),
        in_specs=[spec(smem)] + [spec(vmem)] * 2,
        out_specs=spec(vmem),
        scratch_shapes=fields(8) + [acc_first, tiles_of(blocks), turned],
        compiler_params=params(12),
        cost_estimate=cost(40_000_000),
        name="local_density",
    )(own_items, table, columns)

    density, slopes = pl.pallas_call(
        functools.partial(density_kernel, blocks, faces, per_peer),
        out_shape=(f32(blocks, lanes), f32(3, blocks, lanes)),
        in_specs=[spec(smem)] + [spec(vmem)] * 7,
        out_specs=[spec(vmem)] * 2,
        scratch_shapes=[tiles_of(blocks)],
        compiler_params=params(8),
        name="density",
    )(send_list, table, self_sum, local_sum, far_sum, from_above, from_below, returned)

    force_columns, force_table, pressed, out_low, out_high, out_far = pl.pallas_call(
        functools.partial(far_send_kernel, blocks, faces, per_peer),
        out_shape=(
            columns_shape,
            f32(blocks * 8, lanes),
            f32(blocks, lanes),
            f32(faces * 8, lanes),
            f32(faces * 8, lanes),
            f32(offered * 8, lanes),
        ),
        in_specs=[spec(smem)] * 2 + [spec(vmem)] * 6,
        out_specs=[spec(vmem)] * 6,
        scratch_shapes=[stage, tiles_of(blocks), tiles_of(others)] + fields(10) + [tiles_of(others)],
        compiler_params=params(12),
        cost_estimate=cost(100_000_000),
        name="far_send",
    )(send_list, far_items, table, density, low, high, far, push)

    force_above = to_below(out_low)
    force_below = to_above(out_high)
    force_far = swap_tiles(out_far, tiles)

    own_force = pl.pallas_call(
        functools.partial(own_force_kernel, blocks),
        out_shape=f32(3, blocks, lanes),
        in_specs=[spec(smem)] * 2 + [spec(vmem)] * 3,
        out_specs=spec(vmem),
        scratch_shapes=fields(10) + [acc_first, tiles_of(blocks), turned],
        compiler_params=params(12),
        cost_estimate=cost(80_000_000),
        name="own_force",
    )(self_items, own_items, force_columns, force_table, pressed)

    far_force = pl.pallas_call(
        functools.partial(far_force_kernel, blocks, faces),
        out_shape=f32(3, blocks, lanes),
        in_specs=[spec(smem)] + [spec(vmem)] * 7,
        out_specs=spec(vmem),
        scratch_shapes=[
            tiles_of(others),
            vmem((others, lanes), jnp.float32),
            vmem((others, lanes), jnp.float32),
        ]
        + fields(10)
        + [acc_first, turned],
        compiler_params=params(12),
        cost_estimate=cost(100_000_000),
        name="far_force",
    )(far_items, force_columns, low, high, far, force_below, force_above, force_far)

    acceleration = pl.pallas_call(
        functools.partial(final_kernel, blocks, faces, per_peer),
        out_shape=f32(3, blocks, lanes),
        in_specs=[spec(smem)] + [spec(vmem)] * 10,
        out_specs=spec(vmem),
        scratch_shapes=[tiles_of(blocks)],
        compiler_params=params(8),
        name="total",
    )(
        send_list,
        table,
        density,
        slopes,
        local_sum,
        far_sum,
        own_force,
        far_force,
        force_above,
        force_below,
        force_far,
    )
    return (density, acceleration)


def solution(mesh):
    placed = (
        P(None, ("slab", "tile"), None),
        P(None, ("slab", "tile"), None),
        P(("slab", "tile"), None),
        P(("slab", "tile"), None),
        P(None, ("slab", "tile"), None),
        P(("slab", "tile")),
        P(("slab", "tile")),
        P(("slab", "tile"), None, None),
        P(("slab", "tile"), None),
        P(("slab", "tile"), None),
        P(("slab", "tile")),
    )
    return jax.shard_map(
        on_device,
        mesh=mesh,
        in_specs=placed,
        out_specs=(P(("slab", "tile"), None), P(None, ("slab", "tile"), None)),
        check_vma=False,
    )
```

time: 160 us -> 152 us (0.950)
  starting transfers between devices: 76.5 us -> 42.4 us
  Pallas kernels: 60.9 us -> 78 us
  local copies, waits for them, and re-layouts: 18.5 us -> 27.2 us
    all_to_all x4 -> x3, starting transfers between devices: 53.5 us -> 21.7 us  [swap_tiles(): lax.all_to_all(parts, 'tile', split_axis=0, concat_axis=0, tiled=True)]
    pallas_call x2, Pallas kernels: 13.7 us -> 24.5 us  [the longest x1 14.1 us: on_device(): pl.pallas_call(functools.partial(far_send_kernel, blocks, faces, per_peer...]
    unnamed x65 -> x97, local copies, waits for them, and re-layouts: 18.5 us -> 27.2 us
    pallas_call x1, Pallas kernels: 8.51 us -> 13.1 us  [on_device(): pl.pallas_call(functools.partial(far_force_kernel, blocks, faces), out_sh...]
    pallas_call x1, Pallas kernels: 14.9 us -> 18.5 us  [on_device(): pl.pallas_call(functools.partial(far_density_kernel, blocks, faces), out_...]
    pallas_call x1, Pallas kernels: 8.66 us -> 6 us  [on_device(): pl.pallas_call(functools.partial(local_density_kernel, blocks), out_shape...]
    ppermute x4 -> x3, starting transfers between devices: 15.3 us -> 12.7 us  [to_above(): return lax.ppermute(shard, 'slab', [(i, i + 1) for i in range(count - 1)])]
    pallas_call x1, Pallas kernels: 7.87 us -> 9.97 us  [on_device(): pl.pallas_call(functools.partial(self_density_kernel, blocks), out_shape=...]
  transfers between devices with their start and end apart: 12 -> 9, of which waited for: 0 -> 0; matrix products, arithmetic and copies ran while one was open for 0% -> 0% of each run, Pallas kernels for 19% -> 18%
where the time goes in v1:
time: 152 us; the launch traced here: 149 us
  Pallas kernels  78 us (51%)
  starting transfers between devices  42.4 us (28%)
  local copies, waits for them, and re-layouts  27.2 us (18%)
  between operations  1.59 us (1%)
    unnamed x97, local copies, waits for them, and re-layouts  27.2 us
    all_to_all x3, starting transfers between devices, swap_tiles(): lax.all_to_all(parts, 'tile', split_axis=0, concat_axis=0, tiled=True)  21.7 us
    pallas_call x1, Pallas kernels, on_device(): pl.pallas_call(functools.partial(far_density_kernel, blocks, faces), out_...  18.5 us
    pallas_call x1, Pallas kernels, on_device(): pl.pallas_call(functools.partial(far_send_kernel, blocks, faces, per_peer...  14.1 us
    pallas_call x1, Pallas kernels, on_device(): pl.pallas_call(functools.partial(far_force_kernel, blocks, faces), out_sh...  13.1 us
    ppermute x3, starting transfers between devices, to_above(): return lax.ppermute(shard, 'slab', [(i, i + 1) for i in range(count - 1)])  12.7 us
    pallas_call x1, Pallas kernels, on_device(): pl.pallas_call(functools.partial(own_force_kernel, blocks), out_shape=f32...  10.4 us
    pallas_call x1, Pallas kernels, on_device(): pl.pallas_call(functools.partial(self_density_kernel, blocks), out_shape=...  9.97 us
  transfers between devices with their start and end apart: 9, of which 0 were waited for; matrix products, arithmetic and copies ran while one was open for 0% of the time, Pallas kernels for 18%

profile of v1, /device:TPU:35, one launch (start us, length us, event | category | flops | bytes accessed | tf_op | source)
XLA Modules:
  0.0 149.2 jit_solution(13242907334015227320)
XLA Ops:
  0.6 0.8 copy.14.send
  1.4 0.9 copy-done.23
  2.3 0.9 copy-done.24
  3.2 0.9 copy-done.25
  4.1 0.8 copy-done.32
  4.8 0.8 copy-done.33
  5.6 0.7 copy-done.37
  6.2 0.7 copy-done.39
  6.9 2.0 %pack.1 = (f32[512,128]{1,0:T(8,128)S(1)}, f32[1024,128]{1,0:T(8,128)}, f32[128,128]{1,0:T(8,128)S(1)}, f32[128,128]{1,0:T(8,128)S(1)}) custom-call(s32[1,32,4]{2,1,0:T(8,128)S(1)} %copy.14.send, f32[3,64,128]{2,1,0:T(8,128)S(1)} %copy-done.23, f32[3,64,128]{2,1,0:T(8,128)S(1)} %copy-done.24, f32[64,128]{1,0:T(8,128)S(1)} %copy-done.32, ...), custom_call_target="tpu_custom_call" | custom-call | tf_op jit(solution)/shard_map/pack/pallas_call | solution.py:800
  8.9 10.8 %all-to-all-start = ((f32[32,32,128]{2,1,0:T(8,128)}), f32[32,32,128]{2,1,0:T(8,128)S(1)}, u32[]{:S(2)}, u32[]{:S(2)}) async-start(f32[32,32,128]{2,1,0:T(8,128)} %bitcast.4), calls=%async_computation | async-start | bytes 1048576 | tf_op jit(solution)/shard_map/all_to_all | solution.py:755
  19.7 4.2 %collective-permute-start = (f32[128,128]{1,0:T(8,128)S(1)}, f32[128,128]{1,0:T(8,128)S(1)}, u32[]{:S(2)}, u32[]{:S(2)}) collective-permute-start(f32[128,128]{1,0:T(8,128)S(1)} %get-tuple-element.30), channel_id=1, source_target_pairs={{0,32},{32,64},{64,96},{96,128},{128,160},{160,192},{192,224},{1,3... | collective-permute-start | bytes 196616 | tf_op jit(solution)/shard_map/ppermute | solution.py:745
  23.9 1.9 %collective-permute-start.1 = (f32[128,128]{1,0:T(8,128)S(1)}, f32[128,128]{1,0:T(8,128)S(1)}, u32[]{:S(2)}, u32[]{:S(2)}) collective-permute-start(f32[128,128]{1,0:T(8,128)S(1)} %get-tuple-element.31), channel_id=1, source_target_pairs={{32,0},{64,32},{96,64},{128,96},{160,128},{192,160},{224,192},{33,... | collective-permute-start | bytes 196616 | tf_op jit(solution)/shard_map/ppermute | solution.py:750
  26.5 0.0 copy-start.36
  26.5 0.7 copy-done.36
  27.2 0.7 copy-done.38
  27.8 0.7 copy-done.40
  28.5 0.7 copy-done.43
  29.2 10.0 %self_density.1 = (bf16[65,128,128]{2,1,0:T(8,128)(2,1)S(1)}, f32[64,128]{1,0:T(8,128)S(1)}, s32[280]{0:T(512)S(1)}, s32[560]{0:T(1024)S(1)}, s32[352]{0:T(512)S(1)}) custom-call(s32[64]{0:T(128)S(1)} %copy-done.40, s32[64]{0:T(128)S(1)} %copy-done.38, s32[1]{0:T(128)S(6)} %copy.17.live, s32[2,64]{1,0:T(2,128)S(1)} %bitcast.21, s32[2,160]{1,0:T(2,128)S(1)} %bitcast.18, ...), custom_call_target="tpu_custom_call" | custom-call | flops 40000000 | bytes 400000 | tf_op jit(solution)/shard_map/self_density/pallas_call | solution.py:821
  39.1 0.6 copy-done.41
  39.7 0.0 collective-permute-done.low
  39.7 0.0 all-to-all-done
  39.8 18.5 %far_density.1 = (f32[4,64,128]{2,1,0:T(8,128)S(1)}, f32[64,128]{1,0:T(8,128)S(1)}, f32[64,128]{1,0:T(8,128)S(1)}, f32[512,128]{1,0:T(8,128)S(1)}, f32[3,160,128]{2,1,0:T(8,128)S(1)}, /*index=5*/s32[1328]{0:T(1024)S(1)}) custom-call(s32[352]{0:T(512)S(1)} %get-tuple-element.29.far_pairs, bf16[65,128,128]{2,1,0:T(8,128)(2,1)S(1)} %get-tuple-element.28.columns, ...), custom_call_target="tpu_custom_call" | custom-call | flops 100000000 | bytes 400000 | tf_op jit(solution)/shard_map/far_density/pallas_call | solution.py:838
  58.3 0.7 copy-done.17
  59.0 0.6 copy-done.46
  59.6 0.6 copy-done.47
  60.2 0.7 copy-done.14
  60.9 5.0 %all-to-all-start.1 = ((f32[32,16,128]{2,1,0:T(8,128)}), f32[32,16,128]{2,1,0:T(8,128)S(1)}, u32[]{:S(2)}, u32[]{:S(2)}) async-start(f32[32,16,128]{2,1,0:T(8,128)} %bitcast.17), calls=%async_computation.1 | async-start | bytes 524288 | tf_op jit(solution)/shard_map/all_to_all | solution.py:755
  65.9 4.1 %collective-permute-start.2 = (f32[64,128]{1,0:T(8,128)}, f32[64,128]{1,0:T(8,128)S(1)}, u32[]{:S(2)}, u32[]{:S(2)}) collective-permute-start(f32[64,128]{1,0:T(8,128)} %copy-done.47), channel_id=1, source_target_pairs={{32,0},{64,32},{96,64},{128,96},{160,128},{192,160},{224,192},{33,... | collective-permute-start | bytes 98312 | tf_op jit(solution)/shard_map/ppermute | solution.py:750
  70.0 4.7 %collective-permute-start.3 = (f32[64,128]{1,0:T(8,128)}, f32[64,128]{1,0:T(8,128)S(1)}, u32[]{:S(2)}, u32[]{:S(2)}) collective-permute-start(f32[64,128]{1,0:T(8,128)} %copy-done.46), channel_id=1, source_target_pairs={{0,32},{32,64},{64,96},{96,128},{128,160},{160,192},{192,224},{1,3... | collective-permute-start | bytes 98312 | tf_op jit(solution)/shard_map/ppermute | solution.py:745
  74.7 6.0 %local_density.1.local_sum = f32[4,64,128]{2,1,0:T(8,128)S(1)} custom-call(s32[560]{0:T(1024)S(1)} %get-tuple-element.27.items.both_items, f32[512,128]{1,0:T(8,128)S(1)} %get-tuple-element.25.table, bf16[65,128,128]{2,1,0:T(8,128)(2,1)S(1)} %get-tuple-element.28.columns), custom_call_target="tpu_custom_call" | custom-call | flops 40000000 | bytes 400000 | tf_op jit(solution)/shard_map/local_density/pallas_call | solution.py:868
  80.7 0.0 collective-permute-done.2.from_above
  80.7 0.0 collective-permute-done.3.from_below
  80.7 0.0 copy-start.30
  80.8 0.6 copy-done.30
  81.4 0.0 all-to-all-done.1
  81.4 0.9 copy-done.5
  82.3 0.8 copy-done.31
  83.0 2.0 %density.1 = (f32[64,128]{1,0:T(8,128)}, f32[3,64,128]{2,1,0:T(8,128)S(1)}) custom-call(s32[1,32,4]{2,1,0:T(8,128)S(1)} %copy.14.send, f32[512,128]{1,0:T(8,128)S(1)} %get-tuple-element.25.table, f32[64,128]{1,0:T(8,128)S(1)} %get-tuple-element.26.self_sum, f32[4,64,128]{2,1,0:T(8,128)S(1)} %local_density.1.local_sum, f32[4,64,128]{2,1,0:T(8,128)S(1)} %copy-done.5, ...), custom_call_target="tpu_custom_call" | custom-call | tf_op jit(solution)/shard_map/density/pallas_call | solution.py:879
  85.0 0.6 copy-done.21
  85.7 0.9 copy-done.18
  86.6 0.8 copy-done.19
  87.4 14.1 %far_send.1 = (bf16[65,128,128]{2,1,0:T(8,128)(2,1)S(1)}, f32[512,128]{1,0:T(8,128)S(1)}, f32[64,128]{1,0:T(8,128)S(1)}, f32[128,128]{1,0:T(8,128)S(1)}, f32[128...) custom-call(s32[1,32,4]{2,1,0:T(8,128)S(1)} %copy.14.send, s32[1328]{0:T(1024)S(1)} %get-tuple-element.40.items, ...), custom_call_target="tpu_custom_call" | custom-call | flops 100000000 | bytes 400000 | tf_op jit(solution)/shard_map/far_send/pallas_call | solution.py:889
  101.5 0.7 copy-done.15
  102.2 0.6 copy-done.26
  102.8 0.8 copy-done.7
  103.6 0.0 copy-done.44
  103.6 0.0 copy-done.45
  103.7 6.0 %all-to-all-start.2 = ((f32[32,32,128]{2,1,0:T(8,128)}), f32[32,32,128]{2,1,0:T(8,128)S(1)}, u32[]{:S(2)}, u32[]{:S(2)}) async-start(f32[32,32,128]{2,1,0:T(8,128)} %bitcast.16), calls=%async_computation.2 | async-start | bytes 1048576 | tf_op jit(solution)/shard_map/all_to_all | solution.py:755
  109.6 3.8 %collective-permute-start.4 = (f32[128,128]{1,0:T(8,128)}, f32[128,128]{1,0:T(8,128)S(1)}, u32[]{:S(2)}, u32[]{:S(2)}) collective-permute-start(f32[128,128]{1,0:T(8,128)} %copy-done.45), channel_id=1, source_target_pairs={{0,32},{32,64},{64,96},{96,128},{128,160},{160,192},{192,224},{1,3... | collective-permute-start | bytes 196616 | tf_op jit(solution)/shard_map/ppermute | solution.py:745
  113.5 1.9 %collective-permute-start.5 = (f32[128,128]{1,0:T(8,128)}, f32[128,128]{1,0:T(8,128)S(1)}, u32[]{:S(2)}, u32[]{:S(2)}) collective-permute-start(f32[128,128]{1,0:T(8,128)} %copy-done.44), channel_id=1, source_target_pairs={{32,0},{64,32},{96,64},{128,96},{160,128},{192,160},{224,192},{33,... | collective-permute-start | bytes 196616 | tf_op jit(solution)/shard_map/ppermute | solution.py:750
  115.4 0.9 copy-done.16
  116.4 0.8 copy-done.27
  117.1 0.7 copy-done.35
  117.8 0.7 copy-done.42
  118.5 10.4 %own_force.1 = f32[3,64,128]{2,1,0:T(8,128)S(1)} custom-call(s32[280]{0:T(512)S(1)} %copy-done.42, s32[560]{0:T(1024)S(1)} %copy-done.35, bf16[65,128,128]{2,1,0:T(8,128)(2,1)S(1)} %get-tuple-element.42.columns, f32[512,128]{1,0:T(8,128)S(1)} %copy-done.16, f32[64,128]{1,0:T(8,128)S(1)} %copy-done.27), custom_call_target="tpu_custom_call" | custom-call | flops 80000000 | bytes 400000 | tf_op jit(solution)/shard_map/own_force/pallas_call | solution.py:911
  128.9 0.6 copy-done.8
  129.5 0.6 copy-done.10
  130.1 0.6 copy-done.12
  130.8 0.9 copy-done.3
  131.7 0.8 copy-done.11
  132.5 0.8 copy-done.13
  133.3 0.7 copy-done.29
  134.0 13.1 %far_force.1 = f32[3,64,128]{2,1,0:T(8,128)S(1)} custom-call(s32[1328]{0:T(1024)S(1)} %copy-done.29, bf16[65,128,128]{2,1,0:T(8,128)(2,1)S(1)} %get-tuple-element.42.columns, f32[128,128]{1,0:T(8,128)S(1)} %collective-permute-done.low, f32[128,128]{1,0:T(8,128)S(1)} %copy-done.3, f32[1024,128]{1,0:T(8,128)S(1)} %bitcast.12, f32[128,128]{1,0:T(8,128)S(1)} %copy-done.11, ...), custom_call_target="tpu_custom_call" | custom-call | flops 100000000 | bytes 400000 | tf_op jit(solution)/shard_map/far_force/pallas_call | solution.py:922
  147.2 2.0 %total.1 = f32[3,64,128]{2,1,0:T(8,128)} custom-call(s32[1,32,4]{2,1,0:T(8,128)S(1)} %copy.14.send, f32[512,128]{1,0:T(8,128)S(1)} %get-tuple-element.25.table, f32[64,128]{1,0:T(8,128)S(1)} %copy-done.20, f32[3,64,128]{2,1,0:T(8,128)S(1)} %copy-done.22, f32[4,64,128]{2,1,0:T(8,128)S(1)} %copy-done.1, f32[4,64,128]{2,1,0:T(8,128)S(1)} %copy-done.6, ...), custom_call_target="tpu_custom_call" | custom-call | tf_op jit(solution)/shard_map/total/pallas_call | solution.py:939
  (60 shorter events, 0.1 us)
Async XLA Ops:
  1.4 0.9 copy-start.23
  2.3 0.9 copy-start.24
  3.2 0.9 copy-start.25
  4.1 0.8 copy-start.32
  4.8 0.8 copy-start.33
  5.6 0.7 copy-start.37
  6.2 0.7 copy-start.39
  8.9 30.9 %all-to-all-start = ((f32[32,32,128]{2,1,0:T(8,128)}), f32[32,32,128]{2,1,0:T(8,128)S(1)}, u32[]{:S(2)}, u32[]{:S(2)}) async-start(f32[32,32,128]{2,1,0:T(8,128)} %bitcast.4), calls=%async_computation | async-start | bytes 1048576 | tf_op jit(solution)/shard_map/all_to_all | solution.py:755
  19.7 20.1 %collective-permute-start = (f32[128,128]{1,0:T(8,128)S(1)}, f32[128,128]{1,0:T(8,128)S(1)}, u32[]{:S(2)}, u32[]{:S(2)}) collective-permute-start(f32[128,128]{1,0:T(8,128)S(1)} %get-tuple-element.30), channel_id=1, source_target_pairs={{0,32},{32,64},{64,96},{96,128},{128,160},{160,192},{192,224},{1,3... | collective-permute-start | bytes 196616 | tf_op jit(solution)/shard_map/ppermute | solution.py:745
  23.9 15.8 %collective-permute-start.1 = (f32[128,128]{1,0:T(8,128)S(1)}, f32[128,128]{1,0:T(8,128)S(1)}, u32[]{:S(2)}, u32[]{:S(2)}) collective-permute-start(f32[128,128]{1,0:T(8,128)S(1)} %get-tuple-element.31), channel_id=1, source_target_pairs={{32,0},{64,32},{96,64},{128,96},{160,128},{192,160},{224,192},{33,... | collective-permute-start | bytes 196616 | tf_op jit(solution)/shard_map/ppermute | solution.py:750
  26.5 0.7 copy-start.36
  27.2 0.7 copy-start.38
  27.8 0.7 copy-start.40
  28.5 0.7 copy-start.43
  39.1 0.6 copy-start.41
  39.7 41.0 %copy-start.34 = (s32[560]{0:T(1024)}, s32[560]{0:T(1024)S(1)}, u32[]{:S(2)}) copy-start(s32[560]{0:T(1024)S(1)} %get-tuple-element.27.items.both_items) | copy-start | bytes 6724
  39.7 45.9 %copy-start.2 = (f32[128,128]{1,0:T(8,128)}, f32[128,128]{1,0:T(8,128)S(1)}, u32[]{:S(2)}) copy-start(f32[128,128]{1,0:T(8,128)S(1)} %collective-permute-done.1.high) | copy-start | bytes 196612
  58.3 0.7 copy-start.17
  59.0 0.6 copy-start.46
  59.6 0.6 copy-start.47
  60.2 0.7 copy-start.14
  60.2 14.5 %copy-start.4 = (f32[4,64,128]{2,1,0:T(8,128)}, f32[4,64,128]{2,1,0:T(8,128)S(1)}, u32[]{:S(2)}) copy-start(f32[4,64,128]{2,1,0:T(8,128)S(1)} %get-tuple-element.33.far_sum) | copy-start | bytes 393220
  60.2 41.2 %copy-start.28 = (s32[1328]{0:T(1024)}, s32[1328]{0:T(1024)S(1)}, u32[]{:S(2)}) copy-start(s32[1328]{0:T(1024)S(1)} %get-tuple-element.40.items) | copy-start | bytes 15940
  60.9 20.4 %all-to-all-start.1 = ((f32[32,16,128]{2,1,0:T(8,128)}), f32[32,16,128]{2,1,0:T(8,128)S(1)}, u32[]{:S(2)}, u32[]{:S(2)}) async-start(f32[32,16,128]{2,1,0:T(8,128)} %bitcast.17), calls=%async_computation.1 | async-start | bytes 524288 | tf_op jit(solution)/shard_map/all_to_all | solution.py:755
  65.9 14.8 %collective-permute-start.2 = (f32[64,128]{1,0:T(8,128)}, f32[64,128]{1,0:T(8,128)S(1)}, u32[]{:S(2)}, u32[]{:S(2)}) collective-permute-start(f32[64,128]{1,0:T(8,128)} %copy-done.47), channel_id=1, source_target_pairs={{32,0},{64,32},{96,64},{128,96},{160,128},{192,160},{224,192},{33,... | collective-permute-start | bytes 98312 | tf_op jit(solution)/shard_map/ppermute | solution.py:750
  70.0 10.7 %collective-permute-start.3 = (f32[64,128]{1,0:T(8,128)}, f32[64,128]{1,0:T(8,128)S(1)}, u32[]{:S(2)}, u32[]{:S(2)}) collective-permute-start(f32[64,128]{1,0:T(8,128)} %copy-done.46), channel_id=1, source_target_pairs={{0,32},{32,64},{64,96},{96,128},{128,160},{160,192},{192,224},{1,3... | collective-permute-start | bytes 98312 | tf_op jit(solution)/shard_map/ppermute | solution.py:745
  80.7 22.9 %copy-start = (f32[4,64,128]{2,1,0:T(8,128)}, f32[4,64,128]{2,1,0:T(8,128)S(1)}, u32[]{:S(2)}) copy-start(f32[4,64,128]{2,1,0:T(8,128)S(1)} %local_density.1.local_sum) | copy-start | bytes 393220
  80.7 0.6 copy-start.30
  81.4 0.9 copy-start.5
  82.3 0.8 copy-start.31
  85.0 0.6 copy-start.21
  85.7 0.9 copy-start.18
  86.6 0.8 copy-start.19
  101.5 0.7 copy-start.15
  102.2 0.6 copy-start.26
  102.8 0.8 copy-start.7
  102.8 0.8 copy-start.44
  102.8 0.9 copy-start.45
  103.7 27.1 %all-to-all-start.2 = ((f32[32,32,128]{2,1,0:T(8,128)}), f32[32,32,128]{2,1,0:T(8,128)S(1)}, u32[]{:S(2)}, u32[]{:S(2)}) async-start(f32[32,32,128]{2,1,0:T(8,128)} %bitcast.16), calls=%async_computation.2 | async-start | bytes 1048576 | tf_op jit(solution)/shard_map/all_to_all | solution.py:755
  109.6 19.9 %collective-permute-start.4 = (f32[128,128]{1,0:T(8,128)}, f32[128,128]{1,0:T(8,128)S(1)}, u32[]{:S(2)}, u32[]{:S(2)}) collective-permute-start(f32[128,128]{1,0:T(8,128)} %copy-done.45), channel_id=1, source_target_pairs={{0,32},{32,64},{64,96},{96,128},{128,160},{160,192},{192,224},{1,3... | collective-permute-start | bytes 196616 | tf_op jit(solution)/shard_map/ppermute | solution.py:745
  113.5 16.7 %collective-permute-start.5 = (f32[128,128]{1,0:T(8,128)}, f32[128,128]{1,0:T(8,128)S(1)}, u32[]{:S(2)}, u32[]{:S(2)}) collective-permute-start(f32[128,128]{1,0:T(8,128)} %copy-done.44), channel_id=1, source_target_pairs={{32,0},{64,32},{96,64},{128,96},{160,128},{192,160},{224,192},{33,... | collective-permute-start | bytes 196616 | tf_op jit(solution)/shard_map/ppermute | solution.py:750
  115.4 1.0 copy-start.16
  116.4 0.8 copy-start.27
  117.1 0.7 copy-start.35
  117.8 0.7 copy-start.42
  118.5 28.6 %copy-start.20 = (f32[64,128]{1,0:T(8,128)S(1)}, f32[64,128]{1,0:T(8,128)}, u32[]{:S(2)}) copy-start(f32[64,128]{1,0:T(8,128)} %get-tuple-element.23.density) | copy-start | bytes 98308
  128.9 0.6 copy-start.8
  129.5 0.6 copy-start.10
  130.1 0.6 copy-start.12
  130.8 16.4 %copy-start.1 = (f32[4,64,128]{2,1,0:T(8,128)S(1)}, f32[4,64,128]{2,1,0:T(8,128)}, u32[]{:S(2)}) copy-start(f32[4,64,128]{2,1,0:T(8,128)} %copy-done) | copy-start | bytes 393220
  130.8 0.9 copy-start.3
  131.7 0.8 copy-start.11
  132.5 0.8 copy-start.13
  133.3 0.7 copy-start.29
  134.0 13.1 %copy-start.6 = (f32[4,64,128]{2,1,0:T(8,128)S(1)}, f32[4,64,128]{2,1,0:T(8,128)}, u32[]{:S(2)}) copy-start(f32[4,64,128]{2,1,0:T(8,128)} %copy-done.4) | copy-start | bytes 393220
  134.0 13.1 %copy-start.9 = (f32[3,64,128]{2,1,0:T(8,128)S(1)}, f32[3,64,128]{2,1,0:T(8,128)}, u32[]{:S(2)}) copy-start(f32[3,64,128]{2,1,0:T(8,128)} %copy-done.8) | copy-start | bytes 294916
  134.0 13.1 %copy-start.22 = (f32[3,64,128]{2,1,0:T(8,128)S(1)}, f32[3,64,128]{2,1,0:T(8,128)}, u32[]{:S(2)}) copy-start(f32[3,64,128]{2,1,0:T(8,128)} %copy-done.21) | copy-start | bytes 294916

commit v2 on v1

--- a/solution.py
+++ b/solution.py
@@ -15,8 +15,10 @@
 rows_item = 32
 groups = rows_item // 8
 batch = lanes // rows_item
-halves = 2
+density_halves = 4
+force_halves = 2
 pair_pad = 8
+grant_mib = 64
 bf16 = jnp.bfloat16
 vmem = pltpu.VMEM
 smem = pltpu.SMEM
@@ -118,7 +120,7 @@
 
 
 def close_items(items, count, blocks):
-    for k in range(2 * batch * halves):
+    for k in range(2 * batch * density_halves):
         items[count + k] = jnp.int32(blocks)
 
 
@@ -162,24 +164,26 @@
 
 
 def run_items(columns, spread, wide_fields, tiles, items, start, count, body, finish):
+    halves = wide_fields.shape[0]
+    size = batch * halves
+
     def parts(it):
         for h in range(halves):
             yield h, [decode(items[start + (it * halves + h) * batch + k]) for k in range(batch)]
 
     def prepare(it):
         for h, decoded in parts(it):
-            spread_fields(columns, spread, wide_fields[h], tiles, decoded)
+            spread_fields(columns, spread, wide_fields.at[h], tiles, decoded)
 
     def step(it, carry):
-        done = [(decoded, body(wide_fields[h], decoded)) for h, decoded in parts(it)]
+        done = [(decoded, body(wide_fields.at[h], decoded)) for h, decoded in parts(it)]
         prepare(it + 1)
         for decoded, outs in done:
             finish(decoded, outs)
         return carry
 
     prepare(0)
-    size = batch * halves
-    lax.fori_loop(0, (count + size - 1) >> 3, step, 0)
+    lax.fori_loop(0, (count + size - 1) >> (size.bit_length() - 1), step, 0)
 
 
 def merge_lanes(values, first, lane):
@@ -291,8 +295,7 @@
     far_pairs,
     stage,
     spread,
-    wide_a,
-    wide_b,
+    wide_fields,
     acc_second,
 ):
     make_columns(blocks, table, None, columns, stage)
@@ -307,7 +310,7 @@
     count = lax.fori_loop(0, blocks, self_step, zero, unroll=8)
     close_items(items, count, blocks)
     items[items.shape[0] - 1] = count
-    run_density(columns, spread, (wide_a, wide_b), table, None, acc_second, "self", items, 0, count)
+    run_density(columns, spread, wide_fields, table, None, acc_second, "self", items, 0, count)
     own[...] = plane(acc_second, blocks, 0)
     cap = local_items.shape[0] // 2
 
@@ -356,8 +359,7 @@
     columns,
     own,
     spread,
-    wide_a,
-    wide_b,
+    wide_fields,
     acc_first,
     acc_second,
     turned,
@@ -365,7 +367,7 @@
     make_spread(spread)
     clear(acc_first, 1)
     clear(acc_second, 4)
-    density = functools.partial(run_density, columns, spread, (wide_a, wide_b), table, acc_first, acc_second)
+    density = functools.partial(run_density, columns, spread, wide_fields, table, acc_first, acc_second)
     cap = items.shape[0] // 2
     density("local", items, 0, items[cap - 1])
     density("second", items, cap, items[2 * cap - 1])
@@ -395,8 +397,7 @@
     push,
     items,
     spread,
-    wide_a,
-    wide_b,
+    wide_fields,
     acc_first,
     acc_second,
     turned,
@@ -451,7 +452,7 @@
     items[cap - 1] = n_both
     n_second = lax.fori_loop(0, passes(far_pairs[2 * half - 1]), wall_step, zero)
     close_items(wall_items, n_second, blocks)
-    density = functools.partial(run_density, columns, spread, (wide_a, wide_b), source, acc_first, acc_second)
+    density = functools.partial(run_density, columns, spread, wide_fields, source, acc_first, acc_second)
     density("second", wall_items, 0, n_second)
     density("both", items, 0, n_both)
     density("first", items, cap, n_first - cap)
@@ -591,8 +592,7 @@
     last,
     source,
     spread,
-    wide_a,
-    wide_b,
+    wide_fields,
     acc_second,
 ):
     others = source.shape[0] // 8
@@ -607,7 +607,7 @@
     make_columns(blocks, own_source, last, columns, stage)
     make_spread(spread)
     clear(acc_second, 4)
-    run_force(columns, spread, (wide_a, wide_b), source, None, None, acc_second, "second", items, items.shape[0] // 2)
+    run_force(columns, spread, wide_fields, source, None, None, acc_second, "second", items, items.shape[0] // 2)
     for c in range(3):
         acc_second[pl.ds(4 + c, others, stride=8), :] = push[c] - plane(acc_second, others, 4 + c)
     acc_second[pl.ds(0, faces, stride=8), :] = density[0:faces, :]
@@ -634,8 +634,7 @@
     pressed,
     own,
     spread,
-    wide_a,
-    wide_b,
+    wide_fields,
     acc_first,
     acc_second,
     turned,
@@ -644,7 +643,7 @@
     clear(acc_first, 1)
     clear(acc_second, 4)
     force = functools.partial(
-        run_force, columns, spread, (wide_a, wide_b), source, pressed, acc_first, acc_second
+        run_force, columns, spread, wide_fields, source, pressed, acc_first, acc_second
     )
     force("self", self_items, self_items.shape[0])
     force("local", both_items, both_items.shape[0] // 2)
@@ -669,8 +668,7 @@
     source_density,
     pressed,
     spread,
-    wide_a,
-    wide_b,
+    wide_fields,
     acc_first,
     turned,
 ):
@@ -684,7 +682,7 @@
     force_fields(source, source_density[...], others, pressed)
     make_spread(spread)
     clear(acc_first, 1)
-    run_force(columns, spread, (wide_a, wide_b), source, pressed, acc_first, None, "first", items, items.shape[0] // 2)
+    run_force(columns, spread, wide_fields, source, pressed, acc_first, None, "first", items, items.shape[0] // 2)
     first_rows(acc_first, turned, blocks)
     for c in range(3):
         own[c] = plane(turned, blocks, c)
@@ -777,7 +775,7 @@
     n_local = local_pairs.shape[0]
     n_remote = remote_pairs.shape[0]
     per = lanes // rows_item
-    spare = 3 * batch * halves
+    spare = 3 * batch * density_halves
     self_cap = per * blocks + spare
     own_cap = per * n_local + spare
     far_cap = per * n_remote + spare
@@ -785,8 +783,8 @@
     columns_shape = jax.ShapeDtypeStruct((blocks + 1, lanes, lanes), bf16)
     stage = vmem((blocks * 32, lanes), jnp.float32)
 
-    def fields(number):
-        return [vmem((lanes, 128 * number), bf16)] + [vmem((number, lanes, lanes), jnp.float32)] * 2
+    def fields(number, halves):
+        return [vmem((lanes, 128 * number), bf16), vmem((halves, number, lanes, lanes), jnp.float32)]
 
     acc_first = vmem((blocks // 16 + 1, lanes, lanes), jnp.float32)
     turned = vmem((blocks * 8, lanes), jnp.float32)
@@ -802,7 +800,7 @@
         out_shape=(f32(blocks * 8, lanes), f32(offered * 8, lanes), f32(faces * 8, lanes), f32(faces * 8, lanes)),
         in_specs=[spec(smem)] + [spec(vmem)] * 7,
         out_specs=[spec(vmem)] * 4,
-        compiler_params=params(8),
+        compiler_params=params(grant_mib),
         name="pack",
     )(
         send_list,
@@ -829,8 +827,8 @@
         ),
         in_specs=[spec(smem)] * 5 + [spec(vmem)],
         out_specs=[spec(vmem)] * 2 + [spec(smem)] * 3,
-        scratch_shapes=[stage] + fields(8) + [tiles_of(blocks)],
-        compiler_params=params(12),
+        scratch_shapes=[stage] + fields(8, density_halves) + [tiles_of(blocks)],
+        compiler_params=params(grant_mib),
         cost_estimate=cost(40_000_000),
         name="self_density",
     )(counts, wall_flags, remote_live, local_pairs.T, remote_pairs.T, table)
@@ -847,7 +845,7 @@
         ),
         in_specs=[spec(smem)] + [spec(vmem)] * 4,
         out_specs=[spec(vmem)] * 5 + [spec(smem)],
-        scratch_shapes=fields(8)
+        scratch_shapes=fields(8, density_halves)
         + [acc_first, tiles_of(others), turned]
         + [
             tiles_of(others),
@@ -856,7 +854,7 @@
             smem((far_cap,), jnp.int32),
             pltpu.SemaphoreType.DMA,
         ],
-        compiler_params=params(12),
+        compiler_params=params(grant_mib),
         cost_estimate=cost(100_000_000),
         name="far_density",
     )(far_pairs, columns, low, high, far)
@@ -870,8 +868,8 @@
         out_shape=f32(4, blocks, lanes),
         in_specs=[spec(smem)] + [spec(vmem)] * 2,
         out_specs=spec(vmem),
-        scratch_shapes=fields(8) + [acc_first, tiles_of(blocks), turned],
-        compiler_params=params(12),
+        scratch_shapes=fields(8, density_halves) + [acc_first, tiles_of(blocks), turned],
+        compiler_params=params(grant_mib),
         cost_estimate=cost(40_000_000),
         name="local_density",
     )(own_items, table, columns)
@@ -882,7 +880,7 @@
         in_specs=[spec(smem)] + [spec(vmem)] * 7,
         out_specs=[spec(vmem)] * 2,
         scratch_shapes=[tiles_of(blocks)],
-        compiler_params=params(8),
+        compiler_params=params(grant_mib),
         name="density",
     )(send_list, table, self_sum, local_sum, far_sum, from_above, from_below, returned)
 
@@ -898,8 +896,8 @@
         ),
         in_specs=[spec(smem)] * 2 + [spec(vmem)] * 6,
         out_specs=[spec(vmem)] * 6,
-        scratch_shapes=[stage, tiles_of(blocks), tiles_of(others)] + fields(10) + [tiles_of(others)],
-        compiler_params=params(12),
+        scratch_shapes=[stage, tiles_of(blocks), tiles_of(others)] + fields(10, force_halves) + [tiles_of(others)],
+        compiler_params=params(grant_mib),
         cost_estimate=cost(100_000_000),
         name="far_send",
     )(send_list, far_items, table, density, low, high, far, push)
@@ -913,8 +911,8 @@
         out_shape=f32(3, blocks, lanes),
         in_specs=[spec(smem)] * 2 + [spec(vmem)] * 3,
         out_specs=spec(vmem),
-        scratch_shapes=fields(10) + [acc_first, tiles_of(blocks), turned],
-        compiler_params=params(12),
+        scratch_shapes=fields(10, force_halves) + [acc_first, tiles_of(blocks), turned],
+        compiler_params=params(grant_mib),
         cost_estimate=cost(80_000_000),
         name="own_force",
     )(self_items, own_items, force_columns, force_table, pressed)
@@ -929,9 +927,9 @@
             vmem((others, lanes), jnp.float32),
             vmem((others, lanes), jnp.float32),
         ]
-        + fields(10)
+        + fields(10, force_halves)
         + [acc_first, turned],
-        compiler_params=params(12),
+        compiler_params=params(grant_mib),
         cost_estimate=cost(100_000_000),
         name="far_force",
     )(far_items, force_columns, low, high, far, force_below, force_above, force_far)
@@ -942,7 +940,7 @@
         in_specs=[spec(smem)] + [spec(vmem)] * 10,
         out_specs=spec(vmem),
         scratch_shapes=[tiles_of(blocks)],
-        compiler_params=params(8),
+        compiler_params=params(grant_mib),
         name="total",
     )(
         send_list,

time: 152 us -> 135 us (0.89)
  the two profiles are of different devices: /device:TPU:35 before, /device:TPU:41 now
where the time goes in v2:
time: 135 us; the launch traced here: 133 us
  Pallas kernels  83.1 us (62%)
  starting transfers between devices  47 us (35%)
  between operations  1.41 us (1%)
  local copies, waits for them, and re-layouts  1.36 us (1%)
    all_to_all x3, starting transfers between devices, swap_tiles(): lax.all_to_all(parts, 'tile', split_axis=0, concat_axis=0, tiled=True)  30.4 us
    pallas_call x1, Pallas kernels, on_device(): pl.pallas_call(functools.partial(far_density_kernel, blocks, faces), out_...  16.7 us
    pallas_call x1, Pallas kernels, on_device(): pl.pallas_call(functools.partial(far_send_kernel, blocks, faces, per_peer...  14.1 us
    pallas_call x1, Pallas kernels, on_device(): pl.pallas_call(functools.partial(own_force_kernel, blocks), out_shape=f32...  14 us
    pallas_call x1, Pallas kernels, on_device(): pl.pallas_call(functools.partial(far_force_kernel, blocks, faces), out_sh...  12.9 us
    pallas_call x1, Pallas kernels, on_device(): pl.pallas_call(functools.partial(self_density_kernel, blocks), out_shape=...  10.4 us
    ppermute x3, starting transfers between devices, to_above(): return lax.ppermute(shard, 'slab', [(i, i + 1) for i in range(count - 1)])  9.81 us
    pallas_call x1, Pallas kernels, on_device(): pl.pallas_call(functools.partial(local_density_kernel, blocks), out_shape...  7.51 us
  transfers between devices with their start and end apart: 9, of which 0 were waited for; matrix products, arithmetic and copies ran while one was open for 0% of the time, Pallas kernels for 24%

profile of v2, /device:TPU:41, one launch (start us, length us, event | category | flops | bytes accessed | tf_op | source)
XLA Modules:
  0.0 132.9 jit_solution(2520145003791765393)
XLA Ops:
  0.6 1.4 %copy.14.send = s32[1,32,4]{2,1,0:T(8,128)} copy(s32[1,32,4]{1,2,0:T(4,128)} %param.18) | data formatting | bytes 1024 | tf_op args[7]
  2.0 2.3 %pack.1 = (f32[512,128]{1,0:T(8,128)}, f32[1024,128]{1,0:T(8,128)}, f32[128,128]{1,0:T(8,128)}, f32[128,128]{1,0:T(8,128)}) custom-call(s32[1,32,4]{2,1,0:T(8,128)} %copy.14.send, f32[3,64,128]{2,1,0:T(8,128)} %pos.1, f32[3,64,128]{2,1,0:T(8,128)} %vel.1, f32[64,128]{1,0:T(8,128)} %mass.1, f32[64,128]{1,0:T(8,128)} %area.1, f32[3,64,128]{2,1,0:T(8,128)} %normal.1, ...), custom_call_target="tpu_custom_call" | custom-call | tf_op jit(solution)/shard_map/pack/pallas_call | solution.py:798
  4.3 10.7 %all-to-all-start = ((f32[32,32,128]{2,1,0:T(8,128)}), f32[32,32,128]{2,1,0:T(8,128)}, u32[]{:S(2)}, u32[]{:S(2)}) async-start(f32[32,32,128]{2,1,0:T(8,128)} %bitcast.10), calls=%async_computation | async-start | bytes 1048576 | tf_op jit(solution)/shard_map/all_to_all | solution.py:753
  15.0 4.2 %collective-permute-start = (f32[128,128]{1,0:T(8,128)}, f32[128,128]{1,0:T(8,128)}, u32[]{:S(2)}, u32[]{:S(2)}) collective-permute-start(f32[128,128]{1,0:T(8,128)} %get-tuple-element.30), channel_id=1, source_target_pairs={{0,32},{32,64},{64,96},{96,128},{128,160},{160,192},{192,224},{1,3... | collective-permute-start | bytes 196616 | tf_op jit(solution)/shard_map/ppermute | solution.py:743
  19.3 1.9 %collective-permute-start.1 = (f32[128,128]{1,0:T(8,128)}, f32[128,128]{1,0:T(8,128)}, u32[]{:S(2)}, u32[]{:S(2)}) collective-permute-start(f32[128,128]{1,0:T(8,128)} %get-tuple-element.31), channel_id=1, source_target_pairs={{32,0},{64,32},{96,64},{128,96},{160,128},{192,160},{224,192},{33,... | collective-permute-start | bytes 196616 | tf_op jit(solution)/shard_map/ppermute | solution.py:748
  21.9 10.4 %self_density.1 = (bf16[65,128,128]{2,1,0:T(8,128)(2,1)}, f32[64,128]{1,0:T(8,128)}, s32[304]{0:T(512)}, s32[608]{0:T(1024)}, s32[352]{0:T(512)}) custom-call(s32[64]{0:T(128)} %counts.1, s32[64]{0:T(128)} %flags.1, s32[1]{0:T(128)S(6)} %copy.17.live, s32[2,64]{1,0:T(2,128)} %bitcast.16, s32[2,160]{1,0:T(2,128)} %bitcast.13, f32[512,128]{1,0:T(8,128)} %get-tuple-element.25.table), custom_call_target="tpu_custom_call" | custom-call | flops 40000000 | bytes 400000 | tf_op jit(solution)/shard_map/self_density/pallas_call | solution.py:819
  32.3 0.0 collective-permute-done.low
  32.3 0.0 collective-permute-done.1.high
  32.3 0.0 all-to-all-done
  32.3 16.7 %far_density.1 = (f32[4,64,128]{2,1,0:T(8,128)}, f32[64,128]{1,0:T(8,128)}, f32[64,128]{1,0:T(8,128)}, f32[512,128]{1,0:T(8,128)}, f32[3,160,128]{2,1,0:T(8,128)}, /*index=5*/s32[1376]{0:T(1024)}) custom-call(s32[352]{0:T(512)} %get-tuple-element.29.far_pairs, bf16[65,128,128]{2,1,0:T(8,128)(2,1)} %get-tuple-element.28.columns, ...), custom_call_target="tpu_custom_call" | custom-call | flops 100000000 | bytes 400000 | tf_op jit(solution)/shard_map/far_density/pallas_call | solution.py:836
  49.0 9.5 %all-to-all-start.1 = ((f32[32,16,128]{2,1,0:T(8,128)}), f32[32,16,128]{2,1,0:T(8,128)}, u32[]{:S(2)}, u32[]{:S(2)}) async-start(f32[32,16,128]{2,1,0:T(8,128)} %bitcast.12), calls=%async_computation.1 | async-start | bytes 524288 | tf_op jit(solution)/shard_map/all_to_all | solution.py:753
  58.5 1.9 %collective-permute-start.2 = (f32[64,128]{1,0:T(8,128)}, f32[64,128]{1,0:T(8,128)}, u32[]{:S(2)}, u32[]{:S(2)}) collective-permute-start(f32[64,128]{1,0:T(8,128)} %get-tuple-element.34), channel_id=1, source_target_pairs={{32,0},{64,32},{96,64},{128,96},{160,128},{192,160},{224,192},{33,... | collective-permute-start | bytes 98312 | tf_op jit(solution)/shard_map/ppermute | solution.py:748
  60.5 3.6 %collective-permute-start.3 = (f32[64,128]{1,0:T(8,128)}, f32[64,128]{1,0:T(8,128)}, u32[]{:S(2)}, u32[]{:S(2)}) collective-permute-start(f32[64,128]{1,0:T(8,128)} %get-tuple-element.35), channel_id=1, source_target_pairs={{0,32},{32,64},{64,96},{96,128},{128,160},{160,192},{192,224},{1,3... | collective-permute-start | bytes 98312 | tf_op jit(solution)/shard_map/ppermute | solution.py:743
  64.1 7.5 %local_density.1.local_sum = f32[4,64,128]{2,1,0:T(8,128)} custom-call(s32[608]{0:T(1024)} %get-tuple-element.27.items.both_items, f32[512,128]{1,0:T(8,128)} %get-tuple-element.25.table, bf16[65,128,128]{2,1,0:T(8,128)(2,1)} %get-tuple-element.28.columns), custom_call_target="tpu_custom_call" | custom-call | flops 40000000 | bytes 400000 | tf_op jit(solution)/shard_map/local_density/pallas_call | solution.py:866
  71.6 0.0 collective-permute-done.2.from_above
  71.6 0.0 collective-permute-done.3.from_below
  71.6 0.0 all-to-all-done.1
  71.6 2.4 %density.1 = (f32[64,128]{1,0:T(8,128)}, f32[3,64,128]{2,1,0:T(8,128)}) custom-call(s32[1,32,4]{2,1,0:T(8,128)} %copy.14.send, f32[512,128]{1,0:T(8,128)} %get-tuple-element.25.table, f32[64,128]{1,0:T(8,128)} %get-tuple-element.26.self_sum, f32[4,64,128]{2,1,0:T(8,128)} %local_density.1.local_sum, f32[4,64,128]{2,1,0:T(8,128)} %get-tuple-element.33.far_sum, ...), custom_call_target="tpu_custom_call" | custom-call | tf_op jit(solution)/shard_map/density/pallas_call | solution.py:877
  74.1 14.1 %far_send.1 = (bf16[65,128,128]{2,1,0:T(8,128)(2,1)}, f32[512,128]{1,0:T(8,128)}, f32[64,128]{1,0:T(8,128)}, f32[128,128]{1,0:T(8,128)}, f32[128,128]{1,0:T(8,128)}, /*index=5*/f32[1024,128]{1,0:T(8,128)}) custom-call(s32[1,32,4]{2,1,0:T(8,128)} %copy.14.send, s32[1376]{0:T(1024)} %get-tuple-element.40.items, f32[512,128]{1,0:T(8,128)} %get-tuple-element.25.table, ...), custom_call_target="tpu_custom_call" | custom-call | flops 100000000 | bytes 400000 | tf_op jit(solution)/shard_map/far_send/pallas_call | solution.py:887
  88.2 10.2 %all-to-all-start.2 = ((f32[32,32,128]{2,1,0:T(8,128)}), f32[32,32,128]{2,1,0:T(8,128)}, u32[]{:S(2)}, u32[]{:S(2)}) async-start(f32[32,32,128]{2,1,0:T(8,128)} %bitcast.11), calls=%async_computation.2 | async-start | bytes 1048576 | tf_op jit(solution)/shard_map/all_to_all | solution.py:753
  98.4 1.9 %collective-permute-start.4 = (f32[128,128]{1,0:T(8,128)}, f32[128,128]{1,0:T(8,128)}, u32[]{:S(2)}, u32[]{:S(2)}) collective-permute-start(f32[128,128]{1,0:T(8,128)} %get-tuple-element.45), channel_id=1, source_target_pairs={{0,32},{32,64},{64,96},{96,128},{128,160},{160,192},{192,224},{1,3... | collective-permute-start | bytes 196616 | tf_op jit(solution)/shard_map/ppermute | solution.py:743
  100.3 3.0 %collective-permute-start.5 = (f32[128,128]{1,0:T(8,128)}, f32[128,128]{1,0:T(8,128)}, u32[]{:S(2)}, u32[]{:S(2)}) collective-permute-start(f32[128,128]{1,0:T(8,128)} %get-tuple-element.46), channel_id=1, source_target_pairs={{32,0},{64,32},{96,64},{128,96},{160,128},{192,160},{224,192},{33,... | collective-permute-start | bytes 196616 | tf_op jit(solution)/shard_map/ppermute | solution.py:748
  103.3 14.0 %own_force.1 = f32[3,64,128]{2,1,0:T(8,128)} custom-call(s32[304]{0:T(512)} %get-tuple-element.39.self_items, s32[608]{0:T(1024)} %get-tuple-element.27.items.both_items, bf16[65,128,128]{2,1,0:T(8,128)(2,1)} %get-tuple-element.42.columns, f32[512,128]{1,0:T(8,128)} %get-tuple-element.43.source, f32[64,128]{1,0:T(8,128)} %get-tuple-element.44.pressed), custom_call_target="tpu_custom_call" | custom-call | flops 80000000 | bytes 400000 | tf_op jit(solution)/shard_map/own_force/pallas_call | solution.py:909
  117.3 0.0 collective-permute-done.4.from_below
  117.3 0.0 collective-permute-done.5.from_above
  117.3 0.0 all-to-all-done.2
  117.3 12.9 %far_force.1 = f32[3,64,128]{2,1,0:T(8,128)} custom-call(s32[1376]{0:T(1024)} %get-tuple-element.40.items, bf16[65,128,128]{2,1,0:T(8,128)(2,1)} %get-tuple-element.42.columns, f32[128,128]{1,0:T(8,128)} %collective-permute-done.low, f32[128,128]{1,0:T(8,128)} %collective-permute-done.1.high, f32[1024,128]{1,0:T(8,128)} %bitcast.5.far, ...), custom_call_target="tpu_custom_call" | custom-call | flops 100000000 | bytes 400000 | tf_op jit(solution)/shard_map/far_force/pallas_call | solution.py:920
  130.2 2.7 %total.1 = f32[3,64,128]{2,1,0:T(8,128)} custom-call(s32[1,32,4]{2,1,0:T(8,128)} %copy.14.send, f32[512,128]{1,0:T(8,128)} %get-tuple-element.25.table, f32[64,128]{1,0:T(8,128)} %get-tuple-element.23.density, f32[3,64,128]{2,1,0:T(8,128)} %get-tuple-element.38.slopes, f32[4,64,128]{2,1,0:T(8,128)} %local_density.1.local_sum, ...), custom_call_target="tpu_custom_call" | custom-call | tf_op jit(solution)/shard_map/total/pallas_call | solution.py:937
Async XLA Ops:
  4.3 28.0 %all-to-all-start = ((f32[32,32,128]{2,1,0:T(8,128)}), f32[32,32,128]{2,1,0:T(8,128)}, u32[]{:S(2)}, u32[]{:S(2)}) async-start(f32[32,32,128]{2,1,0:T(8,128)} %bitcast.10), calls=%async_computation | async-start | bytes 1048576 | tf_op jit(solution)/shard_map/all_to_all | solution.py:753
  15.0 17.2 %collective-permute-start = (f32[128,128]{1,0:T(8,128)}, f32[128,128]{1,0:T(8,128)}, u32[]{:S(2)}, u32[]{:S(2)}) collective-permute-start(f32[128,128]{1,0:T(8,128)} %get-tuple-element.30), channel_id=1, source_target_pairs={{0,32},{32,64},{64,96},{96,128},{128,160},{160,192},{192,224},{1,3... | collective-permute-start | bytes 196616 | tf_op jit(solution)/shard_map/ppermute | solution.py:743
  19.3 13.0 %collective-permute-start.1 = (f32[128,128]{1,0:T(8,128)}, f32[128,128]{1,0:T(8,128)}, u32[]{:S(2)}, u32[]{:S(2)}) collective-permute-start(f32[128,128]{1,0:T(8,128)} %get-tuple-element.31), channel_id=1, source_target_pairs={{32,0},{64,32},{96,64},{128,96},{160,128},{192,160},{224,192},{33,... | collective-permute-start | bytes 196616 | tf_op jit(solution)/shard_map/ppermute | solution.py:748
  49.0 22.6 %all-to-all-start.1 = ((f32[32,16,128]{2,1,0:T(8,128)}), f32[32,16,128]{2,1,0:T(8,128)}, u32[]{:S(2)}, u32[]{:S(2)}) async-start(f32[32,16,128]{2,1,0:T(8,128)} %bitcast.12), calls=%async_computation.1 | async-start | bytes 524288 | tf_op jit(solution)/shard_map/all_to_all | solution.py:753
  58.5 13.1 %collective-permute-start.2 = (f32[64,128]{1,0:T(8,128)}, f32[64,128]{1,0:T(8,128)}, u32[]{:S(2)}, u32[]{:S(2)}) collective-permute-start(f32[64,128]{1,0:T(8,128)} %get-tuple-element.34), channel_id=1, source_target_pairs={{32,0},{64,32},{96,64},{128,96},{160,128},{192,160},{224,192},{33,... | collective-permute-start | bytes 98312 | tf_op jit(solution)/shard_map/ppermute | solution.py:748
  60.5 11.2 %collective-permute-start.3 = (f32[64,128]{1,0:T(8,128)}, f32[64,128]{1,0:T(8,128)}, u32[]{:S(2)}, u32[]{:S(2)}) collective-permute-start(f32[64,128]{1,0:T(8,128)} %get-tuple-element.35), channel_id=1, source_target_pairs={{0,32},{32,64},{64,96},{96,128},{128,160},{160,192},{192,224},{1,3... | collective-permute-start | bytes 98312 | tf_op jit(solution)/shard_map/ppermute | solution.py:743
  88.2 29.1 %all-to-all-start.2 = ((f32[32,32,128]{2,1,0:T(8,128)}), f32[32,32,128]{2,1,0:T(8,128)}, u32[]{:S(2)}, u32[]{:S(2)}) async-start(f32[32,32,128]{2,1,0:T(8,128)} %bitcast.11), calls=%async_computation.2 | async-start | bytes 1048576 | tf_op jit(solution)/shard_map/all_to_all | solution.py:753
  98.4 18.9 %collective-permute-start.4 = (f32[128,128]{1,0:T(8,128)}, f32[128,128]{1,0:T(8,128)}, u32[]{:S(2)}, u32[]{:S(2)}) collective-permute-start(f32[128,128]{1,0:T(8,128)} %get-tuple-element.45), channel_id=1, source_target_pairs={{0,32},{32,64},{64,96},{96,128},{128,160},{160,192},{192,224},{1,3... | collective-permute-start | bytes 196616 | tf_op jit(solution)/shard_map/ppermute | solution.py:743
  100.3 17.0 %collective-permute-start.5 = (f32[128,128]{1,0:T(8,128)}, f32[128,128]{1,0:T(8,128)}, u32[]{:S(2)}, u32[]{:S(2)}) collective-permute-start(f32[128,128]{1,0:T(8,128)} %get-tuple-element.46), channel_id=1, source_target_pairs={{32,0},{64,32},{96,64},{128,96},{160,128},{192,160},{224,192},{33,... | collective-permute-start | bytes 196616 | tf_op jit(solution)/shard_map/ppermute | solution.py:748

commit v3 on v2

--- a/solution.py
+++ b/solution.py
@@ -62,7 +62,7 @@
 
     def pick(t, carry):
         for k in range(per_peer):
-            source = pl.multiple_of(send[0, t, k] * 8, 8)
+            source = pl.multiple_of(send[0, k, t] * 8, 8)
             at = pl.multiple_of((t * per_peer + k) * 8, 8)
             picked[pl.ds(at, 8), :] = table[pl.ds(source, 8), :]
         return carry
@@ -82,36 +82,36 @@
 
 
 def make_spread(spread):
-    shape = spread.shape
+    shape = (lanes, spread.shape[1])
     k = lax.broadcasted_iota(jnp.int32, shape, 0) & 31
     tile = lax.broadcasted_iota(jnp.int32, shape, 1) >> 7
     want = jnp.where(tile == 3, 6, jnp.where(tile > 3, tile - 1, tile))
     want = jnp.where(tile == 7, 7, want)
     hit = jnp.logical_and(jnp.logical_and(k < 24, (k & 7) == want), tile < 8)
     hit = jnp.logical_or(hit, jnp.logical_and(jnp.logical_and(k >= 24, k < 27), tile == 8))
-    spread[...] = jnp.where(hit, 1.0, 0.0).astype(bf16)
+    spread[0:lanes, :] = jnp.where(hit, 1.0, 0.0).astype(bf16)
+    lane = lax.broadcasted_iota(jnp.int32, (rows_item, lanes), 1) >> 5
+    for j in range(4):
+        at = lanes + rows_item * j
+        spread[at : at + rows_item, 0:lanes] = jnp.where(lane == j, 1.0, 0.0).astype(bf16)
 
 
 def make_columns(blocks, table, last, columns, stage):
-    lane = lax.broadcasted_iota(jnp.int32, (lanes, lanes), 1) >> 5
-    for g in range(blocks // 4):
-        for j in range(4):
-            b = 4 * g + j
-            for p, piece in enumerate(split3(table[8 * b : 8 * b + 8, :])):
-                stage[32 * b + 8 * p : 32 * b + 8 * p + 8, :] = piece
-            if last is None:
-                stage[32 * b + 24 : 32 * b + 32, :] = jnp.zeros((8, lanes), jnp.float32)
-            else:
-                stage[32 * b + 24 : 32 * b + 32, :] = last[8 * b : 8 * b + 8, :]
+    for b in range(blocks):
+        for p, piece in enumerate(split3(table[8 * b : 8 * b + 8, :])):
+            stage[32 * b + 8 * p : 32 * b + 8 * p + 8, :] = piece
+        if last is None:
+            stage[32 * b + 24 : 32 * b + 32, :] = jnp.zeros((8, lanes), jnp.float32)
+        else:
+            stage[32 * b + 24 : 32 * b + 32, :] = last[8 * b : 8 * b + 8, :]
 
     def some(g, carry):
         turned = stage[pl.ds(pl.multiple_of(g * lanes, lanes), lanes), :].T
-        for j in range(4):
-            columns[g * 4 + j] = jnp.where(lane == j, turned, 0.0).astype(bf16)
+        columns[g] = turned.astype(bf16)
         return carry
 
-    lax.fori_loop(0, blocks // 4, some, 0)
-    columns[blocks] = jnp.zeros((lanes, lanes), bf16)
+    lax.fori_loop(0, blocks // 4, some, 0, unroll=2)
+    columns[blocks // 4] = jnp.zeros((lanes, lanes), bf16)
 
 
 def put_items(items, at, code):
@@ -140,9 +140,13 @@
 
 
 def spread_fields(columns, spread, wide_fields, tiles, decoded):
-    left = jnp.concatenate([columns[first, pl.ds(row, rows_item), :] for first, second, row in decoded], axis=0)
+    parts = []
+    for first, second, row in decoded:
+        mask = spread[pl.ds(pl.multiple_of(lanes + (first & 3) * rows_item, rows_item), rows_item), 0:lanes]
+        parts.append(columns[first >> 2, pl.ds(row, rows_item), :] * mask)
+    left = jnp.concatenate(parts, axis=0)
     for t in range((tiles + 1) // 2):
-        both = jnp.dot(left, spread[:, 256 * t : 256 * t + 256], preferred_element_type=jnp.float32)
+        both = jnp.dot(left, spread[0:lanes, 256 * t : 256 * t + 256], preferred_element_type=jnp.float32)
         wide_fields[2 * t] = both[:, 0:lanes]
         wide_fields[2 * t + 1] = both[:, lanes : 2 * lanes]
 
@@ -288,7 +292,7 @@
     local_pairs,
     remote_pairs,
     table,
-    columns,
+    columns_out,
     own,
     items,
     local_items,
@@ -297,8 +301,12 @@
     spread,
     wide_fields,
     acc_second,
+    columns,
+    sem,
 ):
     make_columns(blocks, table, None, columns, stage)
+    columns_copy = pltpu.make_async_copy(columns, columns_out, sem)
+    columns_copy.start()
     make_spread(spread)
     clear(acc_second, 4)
     zero = jnp.int32(0)
@@ -350,24 +358,30 @@
     for k in range(pair_pad):
         far_pairs[n_fluid + k] = zero
         far_pairs[n_wall + k] = zero
+    columns_copy.wait()
 
 
 def local_density_kernel(
     blocks,
     items,
     table,
-    columns,
+    columns_in,
     own,
     spread,
     wide_fields,
     acc_first,
     acc_second,
     turned,
+    columns,
+    sem,
 ):
+    columns_copy = pltpu.make_async_copy(columns_in, columns, sem)
+    columns_copy.start()
     make_spread(spread)
     clear(acc_first, 1)
     clear(acc_second, 4)
     density = functools.partial(run_density, columns, spread, wide_fields, table, acc_first, acc_second)
+    columns_copy.wait()
     cap = items.shape[0] // 2
     density("local", items, 0, items[cap - 1])
     density("second", items, cap, items[2 * cap - 1])
@@ -386,7 +400,7 @@
     blocks,
     faces,
     far_pairs,
-    columns,
+    columns_in,
     low,
     high,
     far,
@@ -405,19 +419,23 @@
     wall_rows,
     wall_flag,
     wall_items,
+    columns,
     sem,
+    sems,
 ):
     others = source.shape[0] // 8
-    source[0 : faces * 8, :] = low[...]
-    source[faces * 8 : 2 * faces * 8, :] = high[...]
-    source[2 * faces * 8 :, :] = far[...]
+    copies = fetch_source(faces, low, high, far, source, sems)
+    columns_copy = pltpu.make_async_copy(columns_in, columns, sems.at[3])
+    columns_copy.start()
+    make_spread(spread)
+    for copy in copies:
+        copy.wait()
     wall_rows[...] = plane(source, others, 7)
-    copy = pltpu.make_async_copy(wall_rows, wall_flag, sem)
-    copy.start()
-    make_spread(spread)
+    flag_copy = pltpu.make_async_copy(wall_rows, wall_flag, sem)
+    flag_copy.start()
     clear(acc_first, 1)
     clear(acc_second, 4)
-    copy.wait()
+    flag_copy.wait()
     zero = jnp.int32(0)
     half = far_pairs.shape[0] // 2
     cap = items.shape[0] // 2
@@ -452,6 +470,7 @@
     items[cap - 1] = n_both
     n_second = lax.fori_loop(0, passes(far_pairs[2 * half - 1]), wall_step, zero)
     close_items(wall_items, n_second, blocks)
+    columns_copy.wait()
     density = functools.partial(run_density, columns, spread, wide_fields, source, acc_first, acc_second)
     density("second", wall_items, 0, n_second)
     density("both", items, 0, n_both)
@@ -464,6 +483,24 @@
     rows_out(acc_second, back_far, 2 * faces, others - 2 * faces)
     for c in range(3):
         push[c] = plane(acc_second, others, 4 + c)
+
+
+def fetch(pairs, sems):
+    copies = [pltpu.make_async_copy(a, b, sems.at[k]) for k, (a, b) in enumerate(pairs)]
+    for copy in copies:
+        copy.start()
+    return copies
+
+
+def fetch_source(faces, low, high, far, source, sems):
+    return fetch(
+        (
+            (low, source.at[0 : faces * 8]),
+            (high, source.at[faces * 8 : 2 * faces * 8]),
+            (far, source.at[2 * faces * 8 :]),
+        ),
+        sems,
+    )
 
 
 def fluid_mask(blocks, table):
@@ -496,12 +533,12 @@
 
     def give(t, carry):
         for k in range(per_peer):
-            at = pl.multiple_of(send[0, t, k] * 8, 8)
+            at = pl.multiple_of(send[0, k, t] * 8, 8)
             source = pl.multiple_of((t * per_peer + k) * 4, 4)
             total[pl.ds(at, 4), :] += returned[pl.ds(source, 4), :]
         return carry
 
-    lax.fori_loop(0, send.shape[1], give, 0, unroll=2)
+    lax.fori_loop(0, send.shape[2], give, 0, unroll=2)
     density[...] = jnp.where(fluid_mask(blocks, table), kernel_norm * plane(total, blocks, 0), 0.0)
     for c in range(3):
         slopes[c] = plane(total, blocks, 1 + c)
@@ -582,7 +619,7 @@
     high,
     far,
     push,
-    columns,
+    columns_out,
     own_source,
     pressed,
     out_low,
@@ -594,19 +631,23 @@
     spread,
     wide_fields,
     acc_second,
+    columns,
+    sems,
 ):
     others = source.shape[0] // 8
-    source[0 : faces * 8, :] = low[...]
-    source[faces * 8 : 2 * faces * 8, :] = high[...]
-    source[2 * faces * 8 :, :] = far[...]
+    copies = fetch_source(faces, low, high, far, source, sems)
     own_source[...] = table[...]
     press = force_fields(own_source, density[...], blocks, pressed)
     last[...] = jnp.zeros(last.shape, jnp.float32)
     for p, piece in enumerate(split3(press)):
         last[pl.ds(p, blocks, stride=8), :] = piece
     make_columns(blocks, own_source, last, columns, stage)
+    columns_copy = pltpu.make_async_copy(columns, columns_out, sems.at[3])
+    columns_copy.start()
     make_spread(spread)
     clear(acc_second, 4)
+    for copy in copies:
+        copy.wait()
     run_force(columns, spread, wide_fields, source, None, None, acc_second, "second", items, items.shape[0] // 2)
     for c in range(3):
         acc_second[pl.ds(4 + c, others, stride=8), :] = push[c] - plane(acc_second, others, 4 + c)
@@ -616,20 +657,21 @@
     def pick(t, carry):
         for k in range(per_peer):
             at = 8 * (2 * faces + t * per_peer + k)
-            acc_second[pl.ds(at, 1), :] = density[pl.ds(send[0, t, k], 1), :]
+            acc_second[pl.ds(at, 1), :] = density[pl.ds(send[0, k, t], 1), :]
         return carry
 
-    lax.fori_loop(0, send.shape[1], pick, 0, unroll=4)
+    lax.fori_loop(0, send.shape[2], pick, 0, unroll=4)
     out_low[...] = acc_second[0 : 8 * faces, :]
     out_high[...] = acc_second[8 * faces : 16 * faces, :]
     out_far[...] = acc_second[16 * faces :, :]
+    columns_copy.wait()
 
 
 def own_force_kernel(
     blocks,
     self_items,
     both_items,
-    columns,
+    columns_in,
     source,
     pressed,
     own,
@@ -638,10 +680,15 @@
     acc_first,
     acc_second,
     turned,
+    columns,
+    sem,
 ):
+    columns_copy = pltpu.make_async_copy(columns_in, columns, sem)
+    columns_copy.start()
     make_spread(spread)
     clear(acc_first, 1)
     clear(acc_second, 4)
+    columns_copy.wait()
     force = functools.partial(
         run_force, columns, spread, wide_fields, source, pressed, acc_first, acc_second
     )
@@ -656,7 +703,7 @@
     blocks,
     faces,
     items,
-    columns,
+    columns_in,
     low,
     high,
     far,
@@ -671,17 +718,22 @@
     wide_fields,
     acc_first,
     turned,
+    columns,
+    sems,
 ):
     others = source.shape[0] // 8
-    source[0 : faces * 8, :] = low[...]
-    source[faces * 8 : 2 * faces * 8, :] = high[...]
-    source[2 * faces * 8 :, :] = far[...]
+    copies = fetch_source(faces, low, high, far, source, sems)
+    columns_copy = pltpu.make_async_copy(columns_in, columns, sems.at[3])
+    columns_copy.start()
     source_density[0:faces, :] = plane(from_below, faces, 0)
     source_density[faces : 2 * faces, :] = plane(from_above, faces, 0)
     source_density[2 * faces :, :] = plane(returned, others - 2 * faces, 0)
-    force_fields(source, source_density[...], others, pressed)
     make_spread(spread)
     clear(acc_first, 1)
+    for copy in copies:
+        copy.wait()
+    force_fields(source, source_density[...], others, pressed)
+    columns_copy.wait()
     run_force(columns, spread, wide_fields, source, pressed, acc_first, None, "first", items, items.shape[0] // 2)
     first_rows(acc_first, turned, blocks)
     for c in range(3):
@@ -712,12 +764,12 @@
 
     def give(t, carry):
         for k in range(per_peer):
-            at = pl.multiple_of(send[0, t, k] * 8, 8)
+            at = pl.multiple_of(send[0, k, t] * 8, 8)
             source = pl.multiple_of((t * per_peer + k) * 8, 8)
             total[pl.ds(at, 8), :] += returned[pl.ds(source, 8), :]
         return carry
 
-    lax.fori_loop(0, send.shape[1], give, 0, unroll=2)
+    lax.fori_loop(0, send.shape[2], give, 0, unroll=2)
     fluid = fluid_mask(blocks, table)
     mass = plane(table, blocks, 6)
     over_mass = 1.0 / jnp.where(mass > 0.0, mass, 1.0)
@@ -771,6 +823,7 @@
     tiles = lax.axis_size("tile")
     per_peer = send_list.shape[2]
     offered = send_list.shape[1] * per_peer
+    send = jnp.swapaxes(send_list, 1, 2)
     others = 2 * faces + offered
     n_local = local_pairs.shape[0]
     n_remote = remote_pairs.shape[0]
@@ -780,11 +833,12 @@
     own_cap = per * n_local + spare
     far_cap = per * n_remote + spare
     pair_cap = n_remote + 2 * pair_pad
-    columns_shape = jax.ShapeDtypeStruct((blocks + 1, lanes, lanes), bf16)
+    columns_shape = jax.ShapeDtypeStruct((blocks // 4 + 1, lanes, lanes), bf16)
+    columns_scratch = vmem((blocks // 4 + 1, lanes, lanes), bf16)
     stage = vmem((blocks * 32, lanes), jnp.float32)
 
     def fields(number, halves):
-        return [vmem((lanes, 128 * number), bf16), vmem((halves, number, lanes, lanes), jnp.float32)]
+        return [vmem((lanes + 4 * rows_item, 128 * number), bf16), vmem((halves, number, lanes, lanes), jnp.float32)]
 
     acc_first = vmem((blocks // 16 + 1, lanes, lanes), jnp.float32)
     turned = vmem((blocks * 8, lanes), jnp.float32)
@@ -803,7 +857,7 @@
         compiler_params=params(grant_mib),
         name="pack",
     )(
-        send_list,
+        send,
         positions,
         velocities,
         masses,
@@ -826,8 +880,10 @@
             i32(2 * pair_cap),
         ),
         in_specs=[spec(smem)] * 5 + [spec(vmem)],
-        out_specs=[spec(vmem)] * 2 + [spec(smem)] * 3,
-        scratch_shapes=[stage] + fields(8, density_halves) + [tiles_of(blocks)],
+        out_specs=[spec(pl.ANY), spec(vmem)] + [spec(smem)] * 3,
+        scratch_shapes=[stage]
+        + fields(8, density_halves)
+        + [tiles_of(blocks), columns_scratch, pltpu.SemaphoreType.DMA],
         compiler_params=params(grant_mib),
         cost_estimate=cost(40_000_000),
         name="self_density",
@@ -843,7 +899,7 @@
             f32(3, others, lanes),
             i32(2 * far_cap),
         ),
-        in_specs=[spec(smem)] + [spec(vmem)] * 4,
+        in_specs=[spec(smem)] + [spec(pl.ANY)] * 4,
         out_specs=[spec(vmem)] * 5 + [spec(smem)],
         scratch_shapes=fields(8, density_halves)
         + [acc_first, tiles_of(others), turned]
@@ -852,7 +908,9 @@
             vmem((others, lanes), jnp.float32),
             smem((others, lanes), jnp.float32),
             smem((far_cap,), jnp.int32),
+            columns_scratch,
             pltpu.SemaphoreType.DMA,
+            pltpu.SemaphoreType.DMA((4,)),
         ],
         compiler_params=params(grant_mib),
         cost_estimate=cost(100_000_000),
@@ -866,9 +924,10 @@
     local_sum = pl.pallas_call(
         functools.partial(local_density_kernel, blocks),
         out_shape=f32(4, blocks, lanes),
-        in_specs=[spec(smem)] + [spec(vmem)] * 2,
+        in_specs=[spec(smem), spec(vmem), spec(pl.ANY)],
         out_specs=spec(vmem),
-        scratch_shapes=fields(8, density_halves) + [acc_first, tiles_of(blocks), turned],
+        scratch_shapes=fields(8, density_halves)
+        + [acc_first, tiles_of(blocks), turned, columns_scratch, pltpu.SemaphoreType.DMA],
         compiler_params=params(grant_mib),
         cost_estimate=cost(40_000_000),
         name="local_density",
@@ -882,7 +941,7 @@
         scratch_shapes=[tiles_of(blocks)],
         compiler_params=params(grant_mib),
         name="density",
-    )(send_list, table, self_sum, local_sum, far_sum, from_above, from_below, returned)
+    )(send, table, self_sum, local_sum, far_sum, from_above, from_below, returned)
 
     force_columns, force_table, pressed, out_low, out_high, out_far = pl.pallas_call(
         functools.partial(far_send_kernel, blocks, faces, per_peer),
@@ -894,13 +953,13 @@
             f32(faces * 8, lanes),
             f32(offered * 8, lanes),
         ),
-        in_specs=[spec(smem)] * 2 + [spec(vmem)] * 6,
-        out_specs=[spec(vmem)] * 6,
-        scratch_shapes=[stage, tiles_of(blocks), tiles_of(others)] + fields(10, force_halves) + [tiles_of(others)],
+        in_specs=[spec(smem)] * 2 + [spec(vmem)] * 2 + [spec(pl.ANY)] * 3 + [spec(vmem)],
+        out_specs=[spec(pl.ANY)] + [spec(vmem)] * 5,
+        scratch_shapes=[stage, tiles_of(blocks), tiles_of(others)] + fields(10, force_halves) + [tiles_of(others), columns_scratch, pltpu.SemaphoreType.DMA((4,))],
         compiler_params=params(grant_mib),
         cost_estimate=cost(100_000_000),
         name="far_send",
-    )(send_list, far_items, table, density, low, high, far, push)
+    )(send, far_items, table, density, low, high, far, push)
 
     force_above = to_below(out_low)
     force_below = to_above(out_high)
@@ -909,9 +968,10 @@
     own_force = pl.pallas_call(
         functools.partial(own_force_kernel, blocks),
         out_shape=f32(3, blocks, lanes),
-        in_specs=[spec(smem)] * 2 + [spec(vmem)] * 3,
+        in_specs=[spec(smem)] * 2 + [spec(pl.ANY)] + [spec(vmem)] * 2,
         out_specs=spec(vmem),
-        scratch_shapes=fields(10, force_halves) + [acc_first, tiles_of(blocks), turned],
+        scratch_shapes=fields(10, force_halves)
+        + [acc_first, tiles_of(blocks), turned, columns_scratch, pltpu.SemaphoreType.DMA],
         compiler_params=params(grant_mib),
         cost_estimate=cost(80_000_000),
         name="own_force",
@@ -920,7 +980,7 @@
     far_force = pl.pallas_call(
         functools.partial(far_force_kernel, blocks, faces),
         out_shape=f32(3, blocks, lanes),
-        in_specs=[spec(smem)] + [spec(vmem)] * 7,
+        in_specs=[spec(smem)] + [spec(pl.ANY)] * 4 + [spec(vmem)] * 3,
         out_specs=spec(vmem),
         scratch_shapes=[
             tiles_of(others),
@@ -928,7 +988,7 @@
             vmem((others, lanes), jnp.float32),
         ]
         + fields(10, force_halves)
-        + [acc_first, turned],
+        + [acc_first, turned, columns_scratch, pltpu.SemaphoreType.DMA((4,))],
         compiler_params=params(grant_mib),
         cost_estimate=cost(100_000_000),
         name="far_force",
@@ -943,7 +1003,7 @@
         compiler_params=params(grant_mib),
         name="total",
     )(
-        send_list,
+        send,
         table,
         density,
         slopes,

time: 135 us -> 135 us (level)
  the two profiles are of different devices: /device:TPU:41 before, /device:TPU:110 now
where the time goes in v3:
time: 135 us; the launch traced here: 132 us
  Pallas kernels  87.7 us (65%)
  starting transfers between devices  42.9 us (32%)
  between operations  1.47 us (1%)
    all_to_all x3, starting transfers between devices, swap_tiles(): lax.all_to_all(parts, 'tile', split_axis=0, concat_axis=0, tiled=True)  26.9 us
    pallas_call x1, Pallas kernels, on_device(): pl.pallas_call(functools.partial(far_density_kernel, blocks, faces), out_...  18.7 us
    pallas_call x1, Pallas kernels, on_device(): pl.pallas_call(functools.partial(far_force_kernel, blocks, faces), out_sh...  16.9 us
    pallas_call x1, Pallas kernels, on_device(): pl.pallas_call(functools.partial(far_send_kernel, blocks, faces, per_peer...  14.8 us
    pallas_call x1, Pallas kernels, on_device(): pl.pallas_call(functools.partial(own_force_kernel, blocks), out_shape=f32...  14 us
    ppermute x3, starting transfers between devices, to_below(): return lax.ppermute(shard, 'slab', [(i + 1, i) for i in range(count - 1)])  9.21 us
    pallas_call x1, Pallas kernels, on_device(): pl.pallas_call(functools.partial(self_density_kernel, blocks), out_shape=...  9.05 us
    ppermute x3, starting transfers between devices, to_above(): return lax.ppermute(shard, 'slab', [(i, i + 1) for i in range(count - 1)])  6.84 us
  transfers between devices with their start and end apart: 9, of which 0 were waited for; matrix products, arithmetic and copies ran while one was open for 0% of the time, Pallas kernels for 23%

profile of v3, /device:TPU:110, one launch (start us, length us, event | category | flops | bytes accessed | tf_op | source)
XLA Modules:
  0.0 132.1 jit_solution(5426981240346098266)
XLA Ops:
  0.6 2.3 %pack.1 = (f32[512,128]{1,0:T(8,128)}, f32[1024,128]{1,0:T(8,128)}, f32[128,128]{1,0:T(8,128)}, f32[128,128]{1,0:T(8,128)}) custom-call(s32[1,4,32]{2,1,0:T(4,128)} %bitcast.14, f32[3,64,128]{2,1,0:T(8,128)} %pos.1, f32[3,64,128]{2,1,0:T(8,128)} %vel.1, f32[64,128]{1,0:T(8,128)} %mass.1, f32[64,128]{1,0:T(8,128)} %area.1, f32[3,64,128]{2,1,0:T(8,128)} %normal.1, ...), custom_call_target="tpu_custom_call" | custom-call | tf_op jit(solution)/shard_map/pack/pallas_call | solution.py:852
  2.9 10.4 %all-to-all-start = ((f32[32,32,128]{2,1,0:T(8,128)}), f32[32,32,128]{2,1,0:T(8,128)}, u32[]{:S(2)}, u32[]{:S(2)}) async-start(f32[32,32,128]{2,1,0:T(8,128)} %bitcast.11), calls=%async_computation | async-start | bytes 1048576 | tf_op jit(solution)/shard_map/all_to_all | solution.py:805
  13.3 1.9 %collective-permute-start = (f32[128,128]{1,0:T(8,128)}, f32[128,128]{1,0:T(8,128)}, u32[]{:S(2)}, u32[]{:S(2)}) collective-permute-start(f32[128,128]{1,0:T(8,128)} %get-tuple-element.30), channel_id=1, source_target_pairs={{0,32},{32,64},{64,96},{96,128},{128,160},{160,192},{192,224},{1,3... | collective-permute-start | bytes 196616 | tf_op jit(solution)/shard_map/ppermute | solution.py:795
  15.3 3.6 %collective-permute-start.1 = (f32[128,128]{1,0:T(8,128)}, f32[128,128]{1,0:T(8,128)}, u32[]{:S(2)}, u32[]{:S(2)}) collective-permute-start(f32[128,128]{1,0:T(8,128)} %get-tuple-element.31), channel_id=1, source_target_pairs={{32,0},{64,32},{96,64},{128,96},{160,128},{192,160},{224,192},{33,... | collective-permute-start | bytes 196616 | tf_op jit(solution)/shard_map/ppermute | solution.py:800
  19.6 9.0 %self_density.1 = (bf16[17,128,128]{2,1,0:T(8,128)(2,1)}, f32[64,128]{1,0:T(8,128)}, s32[304]{0:T(512)}, s32[608]{0:T(1024)}, s32[352]{0:T(512)}) custom-call(s32[64]{0:T(128)} %counts.1, s32[64]{0:T(128)} %flags.1, s32[1]{0:T(128)S(6)} %copy.13.live, s32[2,64]{1,0:T(2,128)} %bitcast.21, s32[2,160]{1,0:T(2,128)} %bitcast.18, f32[512,128]{1,0:T(8,128)} %get-tuple-element.25.table), custom_call_target="tpu_custom_call" | custom-call | flops 40000000 | bytes 400000 | tf_op jit(solution)/shard_map/self_density/pallas_call | solution.py:873
  28.6 0.0 collective-permute-done.low
  28.6 0.0 collective-permute-done.1.high
  28.7 0.0 all-to-all-done
  28.7 18.7 %far_density.1 = (f32[4,64,128]{2,1,0:T(8,128)}, f32[64,128]{1,0:T(8,128)}, f32[64,128]{1,0:T(8,128)}, f32[512,128]{1,0:T(8,128)}, f32[3,160,128]{2,1,0:T(8,128)}, /*index=5*/s32[1376]{0:T(1024)}) custom-call(s32[352]{0:T(512)} %get-tuple-element.29.far_pairs, bf16[17,128,128]{2,1,0:T(8,128)(2,1)} %get-tuple-element.28.columns_in, ...), custom_call_target="tpu_custom_call" | custom-call | flops 100000000 | bytes 400000 | tf_op jit(solution)/shard_map/far_density/pallas_call | solution.py:892
  47.4 8.2 %all-to-all-start.1 = ((f32[32,16,128]{2,1,0:T(8,128)}), f32[32,16,128]{2,1,0:T(8,128)}, u32[]{:S(2)}, u32[]{:S(2)}) async-start(f32[32,16,128]{2,1,0:T(8,128)} %bitcast.13), calls=%async_computation.1 | async-start | bytes 524288 | tf_op jit(solution)/shard_map/all_to_all | solution.py:805
  55.5 1.9 %collective-permute-start.2 = (f32[64,128]{1,0:T(8,128)}, f32[64,128]{1,0:T(8,128)}, u32[]{:S(2)}, u32[]{:S(2)}) collective-permute-start(f32[64,128]{1,0:T(8,128)} %get-tuple-element.34), channel_id=1, source_target_pairs={{32,0},{64,32},{96,64},{128,96},{160,128},{192,160},{224,192},{33,... | collective-permute-start | bytes 98312 | tf_op jit(solution)/shard_map/ppermute | solution.py:800
  57.4 3.0 %collective-permute-start.3 = (f32[64,128]{1,0:T(8,128)}, f32[64,128]{1,0:T(8,128)}, u32[]{:S(2)}, u32[]{:S(2)}) collective-permute-start(f32[64,128]{1,0:T(8,128)} %get-tuple-element.35), channel_id=1, source_target_pairs={{0,32},{32,64},{64,96},{96,128},{128,160},{160,192},{192,224},{1,3... | collective-permute-start | bytes 98312 | tf_op jit(solution)/shard_map/ppermute | solution.py:795
  60.4 6.8 %local_density.1.local_sum = f32[4,64,128]{2,1,0:T(8,128)} custom-call(s32[608]{0:T(1024)} %get-tuple-element.27.items.both_items, f32[512,128]{1,0:T(8,128)} %get-tuple-element.25.table, bf16[17,128,128]{2,1,0:T(8,128)(2,1)} %get-tuple-element.28.columns_in), custom_call_target="tpu_custom_call" | custom-call | flops 40000000 | bytes 400000 | tf_op jit(solution)/shard_map/local_density/pallas_call | solution.py:924
  67.3 0.0 collective-permute-done.2.from_above
  67.3 0.0 collective-permute-done.3.from_below
  67.3 0.0 all-to-all-done.1
  67.3 2.5 %density.1 = (f32[64,128]{1,0:T(8,128)}, f32[3,64,128]{2,1,0:T(8,128)}) custom-call(s32[1,4,32]{2,1,0:T(4,128)} %bitcast.15, f32[512,128]{1,0:T(8,128)} %get-tuple-element.25.table, f32[64,128]{1,0:T(8,128)} %get-tuple-element.26.self_sum, f32[4,64,128]{2,1,0:T(8,128)} %local_density.1.local_sum, f32[4,64,128]{2,1,0:T(8,128)} %get-tuple-element.33.far_sum, ...), custom_call_target="tpu_custom_call" | custom-call | tf_op jit(solution)/shard_map/density/pallas_call | solution.py:936
  69.8 14.8 %far_send.1 = (bf16[17,128,128]{2,1,0:T(8,128)(2,1)}, f32[512,128]{1,0:T(8,128)}, f32[64,128]{1,0:T(8,128)}, f32[128,128]{1,0:T(8,128)}, f32[128,128]{1,0:T(8,128)}, /*index=5*/f32[1024,128]{1,0:T(8,128)}) custom-call(s32[1,4,32]{2,1,0:T(4,128)} %bitcast.16, s32[1376]{0:T(1024)} %get-tuple-element.40.items, f32[512,128]{1,0:T(8,128)} %get-tuple-element.25.table, ...), custom_call_target="tpu_custom_call" | custom-call | flops 100000000 | bytes 400000 | tf_op jit(solution)/shard_map/far_send/pallas_call | solution.py:946
  84.6 8.3 %all-to-all-start.2 = ((f32[32,32,128]{2,1,0:T(8,128)}), f32[32,32,128]{2,1,0:T(8,128)}, u32[]{:S(2)}, u32[]{:S(2)}) async-start(f32[32,32,128]{2,1,0:T(8,128)} %bitcast.12), calls=%async_computation.2 | async-start | bytes 1048576 | tf_op jit(solution)/shard_map/all_to_all | solution.py:805
  92.9 1.9 %collective-permute-start.4 = (f32[128,128]{1,0:T(8,128)}, f32[128,128]{1,0:T(8,128)}, u32[]{:S(2)}, u32[]{:S(2)}) collective-permute-start(f32[128,128]{1,0:T(8,128)} %get-tuple-element.45), channel_id=1, source_target_pairs={{0,32},{32,64},{64,96},{96,128},{128,160},{160,192},{192,224},{1,3... | collective-permute-start | bytes 196616 | tf_op jit(solution)/shard_map/ppermute | solution.py:795
  94.9 3.6 %collective-permute-start.5 = (f32[128,128]{1,0:T(8,128)}, f32[128,128]{1,0:T(8,128)}, u32[]{:S(2)}, u32[]{:S(2)}) collective-permute-start(f32[128,128]{1,0:T(8,128)} %get-tuple-element.46), channel_id=1, source_target_pairs={{32,0},{64,32},{96,64},{128,96},{160,128},{192,160},{224,192},{33,... | collective-permute-start | bytes 196616 | tf_op jit(solution)/shard_map/ppermute | solution.py:800
  98.5 14.0 %own_force.1 = f32[3,64,128]{2,1,0:T(8,128)} custom-call(s32[304]{0:T(512)} %get-tuple-element.39.self_items, s32[608]{0:T(1024)} %get-tuple-element.27.items.both_items, bf16[17,128,128]{2,1,0:T(8,128)(2,1)} %get-tuple-element.42.columns_in, f32[512,128]{1,0:T(8,128)} %get-tuple-element.43.source, f32[64,128]{1,0:T(8,128)} %get-tuple-element.44.pressed), custom_call_target="tpu_custom_call" | custom-call | flops 80000000 | bytes 400000 | tf_op jit(solution)/shard_map/own_force/pallas_call | solution.py:968
  112.5 0.0 collective-permute-done.4.from_below
  112.5 0.0 collective-permute-done.5.from_above
  112.5 0.0 all-to-all-done.2
  112.5 16.9 %far_force.1 = f32[3,64,128]{2,1,0:T(8,128)} custom-call(s32[1376]{0:T(1024)} %get-tuple-element.40.items, bf16[17,128,128]{2,1,0:T(8,128)(2,1)} %get-tuple-element.42.columns_in, f32[128,128]{1,0:T(8,128)} %collective-permute-done.low, f32[128,128]{1,0:T(8,128)} %collective-permute-done.1.high, f32[1024,128]{1,0:T(8,128)} %bitcast.6.far, ...), custom_call_target="tpu_custom_call" | custom-call | flops 100000000 | bytes 400000 | tf_op jit(solution)/shard_map/far_force/pallas_call | solution.py:980
  129.4 2.7 %total.1 = f32[3,64,128]{2,1,0:T(8,128)} custom-call(s32[1,4,32]{2,1,0:T(4,128)} %bitcast.17, f32[512,128]{1,0:T(8,128)} %get-tuple-element.25.table, f32[64,128]{1,0:T(8,128)} %get-tuple-element.23.density, f32[3,64,128]{2,1,0:T(8,128)} %get-tuple-element.38.slopes, f32[4,64,128]{2,1,0:T(8,128)} %local_density.1.local_sum, ...), custom_call_target="tpu_custom_call" | custom-call | tf_op jit(solution)/shard_map/total/pallas_call | solution.py:997
Async XLA Ops:
  2.9 25.7 %all-to-all-start = ((f32[32,32,128]{2,1,0:T(8,128)}), f32[32,32,128]{2,1,0:T(8,128)}, u32[]{:S(2)}, u32[]{:S(2)}) async-start(f32[32,32,128]{2,1,0:T(8,128)} %bitcast.11), calls=%async_computation | async-start | bytes 1048576 | tf_op jit(solution)/shard_map/all_to_all | solution.py:805
  13.3 15.3 %collective-permute-start = (f32[128,128]{1,0:T(8,128)}, f32[128,128]{1,0:T(8,128)}, u32[]{:S(2)}, u32[]{:S(2)}) collective-permute-start(f32[128,128]{1,0:T(8,128)} %get-tuple-element.30), channel_id=1, source_target_pairs={{0,32},{32,64},{64,96},{96,128},{128,160},{160,192},{192,224},{1,3... | collective-permute-start | bytes 196616 | tf_op jit(solution)/shard_map/ppermute | solution.py:795
  15.3 13.4 %collective-permute-start.1 = (f32[128,128]{1,0:T(8,128)}, f32[128,128]{1,0:T(8,128)}, u32[]{:S(2)}, u32[]{:S(2)}) collective-permute-start(f32[128,128]{1,0:T(8,128)} %get-tuple-element.31), channel_id=1, source_target_pairs={{32,0},{64,32},{96,64},{128,96},{160,128},{192,160},{224,192},{33,... | collective-permute-start | bytes 196616 | tf_op jit(solution)/shard_map/ppermute | solution.py:800
  47.4 20.0 %all-to-all-start.1 = ((f32[32,16,128]{2,1,0:T(8,128)}), f32[32,16,128]{2,1,0:T(8,128)}, u32[]{:S(2)}, u32[]{:S(2)}) async-start(f32[32,16,128]{2,1,0:T(8,128)} %bitcast.13), calls=%async_computation.1 | async-start | bytes 524288 | tf_op jit(solution)/shard_map/all_to_all | solution.py:805
  55.5 11.8 %collective-permute-start.2 = (f32[64,128]{1,0:T(8,128)}, f32[64,128]{1,0:T(8,128)}, u32[]{:S(2)}, u32[]{:S(2)}) collective-permute-start(f32[64,128]{1,0:T(8,128)} %get-tuple-element.34), channel_id=1, source_target_pairs={{32,0},{64,32},{96,64},{128,96},{160,128},{192,160},{224,192},{33,... | collective-permute-start | bytes 98312 | tf_op jit(solution)/shard_map/ppermute | solution.py:800
  57.4 9.8 %collective-permute-start.3 = (f32[64,128]{1,0:T(8,128)}, f32[64,128]{1,0:T(8,128)}, u32[]{:S(2)}, u32[]{:S(2)}) collective-permute-start(f32[64,128]{1,0:T(8,128)} %get-tuple-element.35), channel_id=1, source_target_pairs={{0,32},{32,64},{64,96},{96,128},{128,160},{160,192},{192,224},{1,3... | collective-permute-start | bytes 98312 | tf_op jit(solution)/shard_map/ppermute | solution.py:795
  84.6 27.9 %all-to-all-start.2 = ((f32[32,32,128]{2,1,0:T(8,128)}), f32[32,32,128]{2,1,0:T(8,128)}, u32[]{:S(2)}, u32[]{:S(2)}) async-start(f32[32,32,128]{2,1,0:T(8,128)} %bitcast.12), calls=%async_computation.2 | async-start | bytes 1048576 | tf_op jit(solution)/shard_map/all_to_all | solution.py:805
  92.9 19.6 %collective-permute-start.4 = (f32[128,128]{1,0:T(8,128)}, f32[128,128]{1,0:T(8,128)}, u32[]{:S(2)}, u32[]{:S(2)}) collective-permute-start(f32[128,128]{1,0:T(8,128)} %get-tuple-element.45), channel_id=1, source_target_pairs={{0,32},{32,64},{64,96},{96,128},{128,160},{160,192},{192,224},{1,3... | collective-permute-start | bytes 196616 | tf_op jit(solution)/shard_map/ppermute | solution.py:795
  94.9 17.7 %collective-permute-start.5 = (f32[128,128]{1,0:T(8,128)}, f32[128,128]{1,0:T(8,128)}, u32[]{:S(2)}, u32[]{:S(2)}) collective-permute-start(f32[128,128]{1,0:T(8,128)} %get-tuple-element.46), channel_id=1, source_target_pairs={{32,0},{64,32},{96,64},{128,96},{160,128},{192,160},{224,192},{33,... | collective-permute-start | bytes 196616 | tf_op jit(solution)/shard_map/ppermute | solution.py:800
